TPU v7x, 512 devices: a whole 4x4x16 slice. The times are simulated.
512 devices in a mesh: grp: 8 (over y, x_hi), blk: 64 (over z, x_lo, core).
Axes of the slice: x: 4 (x_hi: 2, x_lo: 2; x = x_hi * 2 + x_lo), y: 4, z: 16, core: 2. Of those that a mesh axis runs over, the one named last changes fastest.
Arguments:
- query_out: bfloat16 [64, 14336], P('blk', 'grp'), may hold values from -6 to 6
- query_in: bfloat16 [64, 8192], P('blk', 'grp'), may hold values from -6 to 6
- basis_out: float32 [14336, 14336], P('grp', 'blk'), may hold values from -0.046875 to 0.046875
- basis_in: float32 [8192, 8192], P('grp', 'blk'), may hold values from -0.0625 to 0.0625
- eigen_out: float32 [14336], replicated, may hold values from 0.05 to 20
- eigen_in: float32 [8192], replicated, may hold values from 0.05 to 20
- panel_index: int32 [2, 64], replicated, may hold values from 0 to 63, each once within a row
- train_out: bfloat16 [32768, 14336], P(('grp', 'blk')), may hold values from -0.046875 to 0.046875
- train_in: bfloat16 [32768, 8192], P(('grp', 'blk')), may hold values from -0.0625 to 0.0625
- train_count: int32 [512], P(('grp', 'blk')), may hold values from 1 to 2, as said below
Outputs:
- scores: float32 [1024, 2], P(('grp', 'blk'))
Inputs may be any that keep to these rules, and one draw needn't show every extreme that they name: Each device's count of live training slots; the first train_count[d] of its 2 slots are live.
All inputs are finite; a program needn't handle non-finite values.
Results may differ from a plain program's by a relative error of at most 0.0003.
Values may be sent and summed in bfloat16 or wider, within the bound.
No kernel may reach another device: no remote copies, remote signals or barrier semaphores. Data moves between devices by JAX's collectives and lax.ppermute only.
A program may use at most 64 MiB of HBM per device.

v0:
```python
import jax
import jax.numpy as jnp
from jax import lax
from jax.sharding import PartitionSpec as P

RANK = 32
NQ = 2
SEQ_DEV = 2


damping = 0.5
highest = lax.Precision.HIGHEST


def panel_scale(eigen_values, panel_order, position, panel_width):
    panel_start = panel_order[position] * panel_width
    picked = lax.dynamic_slice_in_dim(eigen_values, panel_start, panel_width)
    return 1.0 / (picked + damping)


def per_device(
    query_out,
    query_in,
    basis_out,
    basis_in,
    eigen_out,
    eigen_in,
    panel_index,
    train_out,
    train_in,
    train_count,
):
    position = lax.axis_index("blk")
    train_out_wide = train_out.astype(jnp.float32)
    train_in_wide = train_in.astype(jnp.float32)
    gathered_out, gathered_in = (
        lax.all_gather(query_out, "blk", axis=0, tiled=True),
        lax.all_gather(query_in, "blk", axis=0, tiled=True),
    )
    partial_out = jnp.dot(
        gathered_out.astype(jnp.float32),
        basis_out,
        precision=highest,
        preferred_element_type=jnp.float32,
    )
    partial_in = jnp.dot(
        gathered_in.astype(jnp.float32),
        basis_in,
        precision=highest,
        preferred_element_type=jnp.float32,
    )
    rotated_out, rotated_in = lax.psum((partial_out, partial_in), "grp")
    scaled_out = (
        rotated_out * panel_scale(eigen_out, panel_index[0], position, basis_out.shape[1])[None, :]
    )
    scaled_in = (
        rotated_in * panel_scale(eigen_in, panel_index[1], position, basis_in.shape[1])[None, :]
    )
    term_out = jnp.einsum(
        "qp,rp->qr", scaled_out, basis_out, precision=highest, preferred_element_type=jnp.float32
    )
    term_in = jnp.einsum(
        "qp,rp->qr", scaled_in, basis_in, precision=highest, preferred_element_type=jnp.float32
    )
    own_rows = lax.psum_scatter(
        jnp.concatenate([term_out, term_in], axis=1), "blk", scatter_dimension=0, tiled=True
    )
    split_cols = basis_out.shape[0]
    own_out = own_rows[:, :split_cols]
    own_in = own_rows[:, split_cols:]
    full_out, full_in = (
        lax.all_gather(own_out, "grp", axis=1, tiled=True),
        lax.all_gather(own_in, "grp", axis=1, tiled=True),
    )
    message = jnp.concatenate([full_out, full_in], axis=1)
    out_width = full_out.shape[1]
    block_rows = lax.all_gather(message, "blk", axis=0, tiled=True)
    along_out = jnp.einsum(
        "qk,tk->qt",
        block_rows[:, :out_width],
        train_out_wide,
        precision=highest,
        preferred_element_type=jnp.float32,
    )
    along_in = jnp.einsum(
        "qk,tk->qt",
        block_rows[:, out_width:],
        train_in_wide,
        precision=highest,
        preferred_element_type=jnp.float32,
    )
    product = along_out * along_in
    scores = jnp.sum(product.reshape(NQ, RANK, SEQ_DEV, RANK), axis=(1, 3)).T / RANK
    live = jnp.arange(SEQ_DEV, dtype=jnp.int32) < train_count[0]
    return jnp.where(live[:, None], scores, 0.0)


def solution(mesh):
    in_specs = (
        P("blk", "grp"),
        P("blk", "grp"),
        P("grp", "blk"),
        P("grp", "blk"),
        P(),
        P(),
        P(),
        P(("grp", "blk"), None),
        P(("grp", "blk"), None),
        P(("grp", "blk")),
    )
    out_specs = P(("grp", "blk"), None)
    return jax.shard_map(
        per_device, mesh=mesh, in_specs=in_specs, out_specs=out_specs, check_vma=False
    )
```

profile of v0, /device:TPU:1, one launch (start us, length us, event | category | flops | bytes accessed | tf_op | source)
XLA Modules:
  0.0 865.4 jit_solution(16387739890105961976)
XLA Ops:
  6.6 72.7 %all-gather = bf16[64,1,1792]{2,1,0:T(2,128)(2,1)S(1)} all-gather(bf16[1,1,1792]{2,1,0:T(2,128)(2,1)} %bitcast.28), channel_id=1, replica_groups=mesh['grp'=8,'blk'=64] {'blk'}, dimensions={0}, use_global_device_ids=true | all-gather | bytes 232960 | tf_op jit(solution)/shard_map/all_gather | solution.py:37
  79.2 60.5 %all-gather.1 = bf16[64,1,1024]{2,1,0:T(2,128)(2,1)S(1)} all-gather(bf16[1,1,1024]{2,1,0:T(2,128)(2,1)} %bitcast.29), channel_id=1, replica_groups=mesh['grp'=8,'blk'=64] {'blk'}, dimensions={0}, use_global_device_ids=true | all-gather | bytes 133120 | tf_op jit(solution)/shard_map/all_gather | solution.py:38
  139.8 3.0 fusion.7
  142.8 0.9 fusion.10
  143.8 0.7 fusion.20
  147.6 0.8 add_divide_fusion
  149.1 0.8 add_divide_fusion.1
  149.9 81.9 %all-reduce.7.cloned.1.call-done = (f32[64,128]{1,0:T(8,128)}, f32[64,224]{1,0:T(8,128)}) async-done(((f32[64,128]{1,0:T(8,128)}, f32[64,224]{1,0:T(8,128)}), (f32[64,128]{1,0:T(8,128)}, f32[64,224]{1,0:T(8,128)})) %all-reduce.7.cloned.1.call-update) | async-done | bytes 90128 | tf_op jit(solution)/shard_map/psum | solution.py:52
  231.8 2.0 fusion.13
  233.8 0.7 fusion.15
  234.4 0.9 pad_maximum_fusion
  235.4 1.3 dynamic-slice.2
  236.7 413.5 %all-reduce.5.cloned.1.call-done = f32[64,2816]{1,0:T(8,128)} async-done(((f32[64,2816]{1,0:T(8,128)}), f32[64,2816]{1,0:T(8,128)}) %all-reduce.5.cloned.1.call-update) | async-done | bytes 720912
  650.2 1.5 constant_dynamic-slice_fusion.2
  651.6 28.2 %all_gather.17 = f32[1,14336]{1,0:T(1,128)S(1)} all-gather(f32[1,1792]{1,0:T(1,128)S(1)} %constant_dynamic-slice_fusion.2), channel_id=1, replica_groups=mesh['grp'=8,'blk'=64] {'grp'}, dimensions={1}, use_global_device_ids=true | all-gather | bytes 64512 | tf_op jit(solution)/shard_map/all_gather | solution.py:72
  679.9 1.5 dynamic-slice.5
  681.4 27.7 %all_gather.18 = f32[1,8192]{1,0:T(1,128)S(1)} all-gather(f32[1,1024]{1,0:T(1,128)S(1)} %dynamic-slice.5), channel_id=1, replica_groups=mesh['grp'=8,'blk'=64] {'grp'}, dimensions={1}, use_global_device_ids=true | all-gather | bytes 36864 | tf_op jit(solution)/shard_map/all_gather | solution.py:73
  709.1 0.7 maximum_bitcast_fusion
  710.5 140.1 %all-gather.5.cloned.1.call-done = f32[64,1,22528]{2,1,0:T(1,128)} async-done(((f32[1,1,22528]{2,1,0:T(1,128)}), f32[64,1,22528]{2,1,0:T(1,128)}) %all-gather.5.cloned.1.call-update) | async-done | bytes 5767184 | tf_op jit(solution)/shard_map/all_gather | solution.py:77
  850.6 4.4 copy.24
  854.9 1.1 fusion.2
  856.1 1.9 fusion.4
  858.1 0.1 reduce_sum.9
  858.2 0.7 copy.11
  (24 shorter events, 0.3 us)
Async XLA Ops:
  6.5 849.5 %copy-start = (bf16[64,14336]{1,0:T(8,128)(2,1)S(1)}, bf16[64,14336]{1,0:T(8,128)(2,1)}, u32[]{:S(2)}) copy-start(bf16[64,14336]{1,0:T(8,128)(2,1)} %param.17) | copy-start | bytes 5505028
  6.5 225.2 %copy-start.1 = (f32[1792,224]{0,1:T(8,128)S(1)}, f32[1792,224]{0,1:T(8,128)}, u32[]{:S(2)}) copy-start(f32[1792,224]{0,1:T(8,128)} %param.12) | copy-start | bytes 4816900
  6.5 137.3 %copy-start.6 = (s32[2,64]{1,0:T(2,128)S(1)}, s32[2,64]{1,0:T(2,128)}, u32[]{:S(2)}) copy-start(s32[2,64]{1,0:T(2,128)} %param.16) | copy-start | bytes 1540
  6.5 225.2 %all-reduce.7.cloned.1.call-start = ((), (), s32[]{:S(2)}) async-start(), calls=%async_computation.2 | async-start | bytes 196608 | tf_op jit(solution)/shard_map/psum | solution.py:52
  6.5 136.2 %copy-start.2 = (f32[1024,128]{1,0:T(8,128)S(1)}, f32[1024,128]{1,0:T(8,128)}, u32[]{:S(2)}) copy-start(f32[1024,128]{1,0:T(8,128)} %param.13) | copy-start | bytes 1572868
  143.7 506.4 %all-reduce.5.cloned.1.call-start = ((), (), s32[]{:S(2)}) async-start(), calls=%async_computation.1 | async-start | bytes 1441792
  231.8 2.0 copy-start.3
  231.8 2.0 copy-start.5
  235.4 615.2 %all-gather.5.cloned.1.call-start = ((), (), s32[]{:S(2)}) async-start(), calls=%async_computation | async-start | bytes 5857280 | tf_op jit(solution)/shard_map/all_gather | solution.py:77
  710.5 144.4 %copy-start.4 = (bf16[64,8192]{1,0:T(8,128)(2,1)S(1)}, bf16[64,8192]{1,0:T(8,128)(2,1)}, u32[]{:S(2)}) copy-start(bf16[64,8192]{1,0:T(8,128)(2,1)} %param.18) | copy-start | bytes 3145732
Sparse Core Ops, SparseCore 0:
  143.9 87.8 all-reduce.6
  235.5 414.6 all-reduce.4
  710.0 140.5 all-gather.4
where the time goes:
time: 866 us; the launch traced here: 865 us
  waiting for transfers between devices  636 us (73%)
  blocking collectives  189 us (22%)
  between operations  17.7 us (2%)
  matrix products  9.56 us (1%)
  local copies, waits for them, and re-layouts  9.37 us (1%)
    unnamed x4, waiting for transfers between devices  414 us
    all_gather x1, waiting for transfers between devices, per_device(): block_rows = lax.all_gather(message, 'blk', axis=0, tiled=True)  140 us
    psum x1, waiting for transfers between devices, per_device(): rotated_out, rotated_in = lax.psum((partial_out, partial_in), 'grp')  81.9 us
    all_gather x1, blocking collectives, per_device(): lax.all_gather(query_out, 'blk', axis=0, tiled=True)  72.7 us
    all_gather x1, blocking collectives, per_device(): lax.all_gather(query_in, 'blk', axis=0, tiled=True)  60.5 us
    all_gather x1, blocking collectives, per_device(): lax.all_gather(own_out, 'grp', axis=1, tiled=True)  28.2 us
    all_gather x1, blocking collectives, per_device(): lax.all_gather(own_in, 'grp', axis=1, tiled=True)  27.7 us
  transfers between devices with their start and end apart: 3, of which 3 were waited for; matrix products, arithmetic and copies ran while one was open for 0% of the time, Pallas kernels for 0%

commit v1 on v0

v1 whole, which is shorter than its diff:
```python
import functools

import jax
import jax.numpy as jnp
from jax import lax
from jax.experimental import pallas as pl
from jax.experimental.pallas import tpu as pltpu
from jax.sharding import Mesh
from jax.sharding import PartitionSpec as P

NQ = 2
SEQ_DEV = 2
RANK = 32
DAMPING = 0.5
LANES = 128
SLOTS = 24
STEPS = 8
TOP = 32766.0
GRP = ("y", "xh")
BLK = ("z", "xl", "c")
VMEM_LIMIT = 48 * 1024 * 1024

f32 = jnp.float32
bf16 = jnp.bfloat16


def split2(x):
    hi = x.astype(bf16)
    return hi, (x - hi.astype(f32)).astype(bf16)


def dot_nn(a, b):
    return lax.dot_general(a, b, (((1,), (0,)), ((), ())), preferred_element_type=f32)


def dot_nt(a, b):
    return lax.dot_general(a, b, (((1,), (1,)), ((), ())), preferred_element_type=f32)


def call(body, out_shape, scratch=(), n_in=1, smem=()):
    specs = [
        pl.BlockSpec(memory_space=pltpu.SMEM if i in smem else pltpu.VMEM) for i in range(n_in)
    ]
    outs = jax.tree.map(lambda _: pl.BlockSpec(memory_space=pltpu.VMEM), out_shape)
    return pl.pallas_call(
        body,
        out_shape=out_shape,
        in_specs=specs,
        out_specs=outs,
        scratch_shapes=list(scratch),
        compiler_params=pltpu.CompilerParams(vmem_limit_bytes=VMEM_LIMIT),
    )


def rotate_body(n_out, n_in, q_ref, bto_ref, bi_ref, part_ref, wide, rows):
    n = q_ref.shape[0]
    wide[...] = q_ref[...].astype(f32).reshape(wide.shape)
    for r in range(n_out + n_in):
        rows[:, r * LANES : (r + 1) * LANES] = wide[pl.ds(r, n, stride=SLOTS), :].astype(bf16)
    w_out = bto_ref.shape[0]
    q_out = rows[:, : n_out * LANES]
    q_in = rows[:, n_out * LANES :]
    hi, lo = split2(bto_ref[...])
    part_ref[...] = jnp.zeros_like(part_ref)
    part_ref[:, :w_out] = dot_nt(q_out, hi) + dot_nt(q_out, lo)
    hi, lo = split2(bi_ref[...])
    part_ref[:, part_ref.shape[1] - bi_ref.shape[1] :] = dot_nn(q_in, hi) + dot_nn(q_in, lo)


def restore_body(core_ref, part_ref, scale_ref, bto_ref, bi_ref, keep_ref, send_ref, coords):
    total = part_ref[0]
    for g in range(1, part_ref.shape[0]):
        total = total + part_ref[g]
    coords[...] = total * scale_ref[...]
    half = keep_ref.shape[0]
    core = core_ref[0]
    mine = coords[pl.ds(pl.multiple_of(core * half, half), half), :]
    other = coords[pl.ds(pl.multiple_of((1 - core) * half, half), half), :]
    both = jnp.concatenate([mine, other], axis=0)
    w_out, k_out = bto_ref.shape
    w_in = bi_ref.shape[1]
    hi, lo = split2(both[:, :w_out])
    b_hi, b_lo = split2(bto_ref[...])
    term = dot_nn(hi, b_hi) + dot_nn(hi, b_lo) + dot_nn(lo, b_hi)
    keep_ref[:, :k_out] = term[:half]
    send_ref[:, :k_out] = term[half:]
    hi, lo = split2(both[:, both.shape[1] - w_in :])
    b_hi, b_lo = split2(bi_ref[...])
    term = dot_nt(hi, b_hi) + dot_nt(hi, b_lo) + dot_nt(lo, b_hi)
    keep_ref[:, k_out:] = term[:half]
    send_ref[:, k_out:] = term[half:]


def level(top):
    return jnp.ceil(STEPS * jnp.log2(jnp.maximum(top, 1e-30)))


def unit(steps):
    return jnp.exp2(steps * (1.0 / STEPS)) * (1.0 / TOP)


def encode_rows_body(n_out, n_in, keep_ref, got_ref, code_ref, wide):
    n = keep_ref.shape[0]
    for first, count, row in ((0, n_out, n_out + n_in), (n_out, n_in, n_out + n_in + 1)):
        x = (
            keep_ref[:, first * LANES : (first + count) * LANES]
            + got_ref[:, first * LANES : (first + count) * LANES]
        )
        steps = level(jnp.max(jnp.abs(x), axis=1, keepdims=True))
        codes = jnp.round(x * (1.0 / unit(steps)))
        for r in range(count):
            wide[pl.ds(first + r, n, stride=SLOTS), :] = codes[:, r * LANES : (r + 1) * LANES]
        wide[pl.ds(row, n, stride=SLOTS), :] = jnp.broadcast_to(steps, (n, LANES))
    code_ref[...] = wide[...].astype(jnp.int32).astype(jnp.int16).reshape(code_ref.shape)


def sum_codes_body(n_out, n_in, code_ref, out_ref):
    slot = lax.broadcasted_iota(jnp.int32, (SLOTS, LANES), 0)
    is_out = slot < n_out
    is_in = jnp.logical_and(slot >= n_out, slot < n_out + n_in)
    total = jnp.zeros((SLOTS, LANES), f32)
    for j in range(code_ref.shape[0]):
        x = code_ref[j].astype(jnp.int32).astype(f32)
        a = x[n_out + n_in : n_out + n_in + 1]
        b = x[n_out + n_in + 1 : n_out + n_in + 2]
        total = total + x * unit(jnp.where(is_out, a, b))
    size = jnp.abs(total)
    steps_out = level(jnp.max(jnp.where(is_out, size, 0.0), keepdims=True))
    steps_in = level(jnp.max(jnp.where(is_in, size, 0.0), keepdims=True))
    steps = jnp.where(is_out, steps_out, steps_in)
    codes = jnp.round(total * (1.0 / unit(steps)))
    codes = jnp.where(slot == n_out + n_in, steps_out, codes)
    codes = jnp.where(slot == n_out + n_in + 1, steps_in, codes)
    codes = codes.astype(jnp.int32).astype(jnp.int16)
    for j in range(out_ref.shape[0]):
        out_ref[j] = codes


def score_body(n_out, n_in, groups, live_ref, code_ref, to_ref, ti_ref, out_ref, wide, hi, lo):
    n = code_ref.shape[0] // groups
    along_out = jnp.zeros((to_ref.shape[0], n), f32)
    along_in = jnp.zeros((ti_ref.shape[0], n), f32)
    for g in range(groups):
        x = code_ref[g * n : (g + 1) * n].astype(jnp.int32).astype(f32)
        wide[...] = x.reshape(wide.shape)
        for first, count, row in ((0, n_out, n_out + n_in), (n_out, n_in, n_out + n_in + 1)):
            scale = unit(wide[pl.ds(row, n, stride=SLOTS), :])
            for r in range(count):
                v = wide[pl.ds(first + r, n, stride=SLOTS), :] * scale
                a, b = split2(v)
                hi[:, r * LANES : (r + 1) * LANES] = a
                lo[:, r * LANES : (r + 1) * LANES] = b
            width = count * LANES
            t_ref = to_ref if first == 0 else ti_ref
            t = t_ref[:, g * width : (g + 1) * width]
            part = dot_nt(t, hi[:, :width]) + dot_nt(t, lo[:, :width])
            if first == 0:
                along_out = along_out + part
            else:
                along_in = along_in + part
    product = along_out * along_in
    rows = product.shape[0]
    q_id = lax.rem(lax.broadcasted_iota(jnp.int32, (rows, n), 1), 16) // 8
    s_id = lax.broadcasted_iota(jnp.int32, (rows, n), 0) // RANK
    row = lax.broadcasted_iota(jnp.int32, out_ref.shape, 0)
    col = lax.broadcasted_iota(jnp.int32, out_ref.shape, 1)
    result = jnp.zeros(out_ref.shape, f32)
    for s in range(SEQ_DEV):
        for q in range(NQ):
            picked = jnp.where(jnp.logical_and(s_id == s, q_id == q), product, 0.0)
            value = jnp.sum(picked) * (1.0 / RANK)
            value = jnp.where(live_ref[0] > s, value, 0.0)
            result = jnp.where(jnp.logical_and(row == s, col == q), value, result)
    out_ref[...] = result


def panel_scale(eigen_values, panel, width):
    picked = lax.dynamic_slice_in_dim(eigen_values, panel * width, width)
    return 1.0 / (picked + DAMPING)


def per_device(qo, qi, bo, bi, eo, ei, panels, to, ti, live):
    n_out, n_in = qo.shape[1] // LANES, qi.shape[1] // LANES
    data = n_out + n_in
    nz, nxl, nc = (lax.axis_size(a) for a in BLK)
    n_grp = lax.axis_size(GRP)
    n_rows = nz * nxl * nc
    half = n_rows // nc
    position = lax.axis_index(BLK)
    w_out, w_in = bo.shape[1], bi.shape[1]
    w_pad = -(-w_out // LANES) * LANES
    bto = bo.T

    own = jnp.concatenate([qo, qi], axis=1).reshape(data, LANES)
    own = jnp.pad(own, ((0, SLOTS - data), (0, 0)))
    spread = jnp.broadcast_to(own[None], (nz * nxl, SLOTS, LANES))
    got = lax.all_to_all(spread, ("z", "xl"), split_axis=0, concat_axis=0, tiled=True)
    queries = lax.all_gather(got, "c", axis=0, tiled=True)

    part = call(
        functools.partial(rotate_body, n_out, n_in),
        jax.ShapeDtypeStruct((n_rows, w_pad + w_in), f32),
        [pltpu.VMEM((n_rows * SLOTS, LANES), f32), pltpu.VMEM((n_rows, data * LANES), bf16)],
        n_in=3,
    )(queries, bto, bi)
    parts = lax.all_to_all(
        jnp.broadcast_to(part[None], (n_grp, *part.shape)), GRP, split_axis=0, concat_axis=0
    )

    scale = jnp.concatenate(
        [
            panel_scale(eo, panels[0, position], w_out),
            jnp.zeros((w_pad - w_out,), f32),
            panel_scale(ei, panels[1, position], w_in),
        ]
    )[None]
    core = lax.axis_index("c").astype(jnp.int32)[None]
    block = jax.ShapeDtypeStruct((half, data * LANES), f32)
    keep, send = call(
        restore_body,
        (block, block),
        [pltpu.VMEM((n_rows, w_pad + w_in), f32)],
        n_in=5,
        smem=(0,),
    )(core, parts, scale, bto, bi)
    other = lax.ppermute(send, "c", [(0, 1), (1, 0)])
    codes = call(
        functools.partial(encode_rows_body, n_out, n_in),
        jax.ShapeDtypeStruct((half, SLOTS, LANES), jnp.int16),
        [pltpu.VMEM((half * SLOTS, LANES), f32)],
        n_in=2,
    )(keep, other)
    codes = lax.all_to_all(codes, ("z", "xl"), split_axis=0, concat_axis=0, tiled=True)
    codes = call(
        functools.partial(sum_codes_body, n_out, n_in),
        jax.ShapeDtypeStruct((nz, SLOTS, LANES), jnp.int16),
    )(codes)
    codes = lax.all_to_all(codes, "z", split_axis=0, concat_axis=0, tiled=True)
    codes = lax.all_gather(codes, ("y", "xh", "xl", "c"), axis=0, tiled=True)
    return call(
        functools.partial(score_body, n_out, n_in, n_grp),
        jax.ShapeDtypeStruct((SEQ_DEV, NQ), f32),
        [
            pltpu.VMEM((n_rows * SLOTS, LANES), f32),
            pltpu.VMEM((n_rows, n_out * LANES), bf16),
            pltpu.VMEM((n_rows, n_out * LANES), bf16),
        ],
        n_in=4,
        smem=(0,),
    )(live, codes, to, ti)


def solution(mesh):
    fine = Mesh(mesh.devices.reshape(4, 2, 16, 2, 2), GRP + BLK)
    in_specs = (
        P(BLK, GRP),
        P(BLK, GRP),
        P(GRP, BLK),
        P(GRP, BLK),
        P(),
        P(),
        P(),
        P(GRP + BLK, None),
        P(GRP + BLK, None),
        P(GRP + BLK),
    )
    out_specs = P(GRP + BLK, None)
    return jax.shard_map(
        per_device, mesh=fine, in_specs=in_specs, out_specs=out_specs, check_vma=False
    )
```

time: 866 us -> 140 us (0.16)
  waiting for transfers between devices: 636 us -> 22.4 us
  blocking collectives: 189 us -> 88.3 us
  between operations: 17.7 us -> 1.98 us
  starting transfers between devices: 0.09 us -> 13.6 us
  matrix products: 9.56 us -> 0 us
    unnamed x4 -> x0, waiting for transfers between devices: 414 us -> none
    all_gather x4 -> x2, blocking collectives: 189 us -> 32.9 us  [the longest x1 27.9 us: per_device(): codes = lax.all_gather(codes, ('y', 'xh', 'xl', 'c'), axis=0, tiled=True)]
    all_gather x1 -> x0, waiting for transfers between devices: 140 us -> none  [per_device(): block_rows = lax.all_gather(message, 'blk', axis=0, tiled=True)]
    psum x1 -> x0, waiting for transfers between devices: 81.9 us -> none  [per_device(): rotated_out, rotated_in = lax.psum((partial_out, partial_in), 'grp')]
    all_to_all x0 -> x2, blocking collectives: none -> 55.4 us  [the longest x1 33.6 us: per_device(): lax.all_to_all(spread, ('z', 'xl'), split_axis=0, concat_axis=0, tiled=True)]
    all_to_all x0 -> x2, waiting for transfers between devices: none -> 21.1 us  [the longest x1 11.1 us: per_device(): codes = lax.all_to_all(codes, 'z', split_axis=0, concat_axis=0, tiled=True)]
    all_to_all x0 -> x2, starting transfers between devices: none -> 9.86 us  [the longest x1 6.36 us: per_device(): lax.all_to_all(jnp.broadcast_to(part[None], (n_grp, *part.shape)), GRP, s...]
    dot_general x6 -> x0, matrix products: 9.56 us -> none  [the longest x1 3.01 us: per_device(): jnp.dot(gathered_out.astype(jnp.float32), basis_out, precision=highest, p...]
  transfers between devices with their start and end apart: 3 -> 3, of which waited for: 3 -> 3; matrix products, arithmetic and copies ran while one was open for 0% -> 2% of each run, Pallas kernels for 0% -> 0%
where the time goes in v1:
time: 140 us
  blocking collectives  88.3 us (63%)
  waiting for transfers between devices  22.4 us (16%)
  starting transfers between devices  13.6 us (10%)
  Pallas kernels  7.09 us (5%)
  local copies, waits for them, and re-layouts  4.13 us (3%)
  other arithmetic  2.38 us (2%)
  between operations  1.98 us (1%)
    all_to_all x1, blocking collectives, per_device(): lax.all_to_all(spread, ('z', 'xl'), split_axis=0, concat_axis=0, tiled=True)  33.6 us
    all_gather x1, blocking collectives, per_device(): codes = lax.all_gather(codes, ('y', 'xh', 'xl', 'c'), axis=0, tiled=True)  27.9 us
    all_to_all x1, blocking collectives, per_device(): lax.all_to_all(codes, ('z', 'xl'), split_axis=0, concat_axis=0, tiled=True)  21.8 us
    all_to_all x1, waiting for transfers between devices, per_device(): codes = lax.all_to_all(codes, 'z', split_axis=0, concat_axis=0, tiled=True)  11.1 us
    all_to_all x1, waiting for transfers between devices, per_device(): lax.all_to_all(jnp.broadcast_to(part[None], (n_grp, *part.shape)), GRP, s...  9.99 us
    all_to_all x1, starting transfers between devices, per_device(): lax.all_to_all(jnp.broadcast_to(part[None], (n_grp, *part.shape)), GRP, s...  6.36 us
    all_gather x1, blocking collectives, per_device(): queries = lax.all_gather(got, 'c', axis=0, tiled=True)  4.96 us
    pallas_call x1, Pallas kernels, per_device(): call(functools.partial(score_body, n_out, n_in, n_grp), jax.ShapeDtypeStr...  4.44 us
  transfers between devices with their start and end apart: 3, of which 3 were waited for; matrix products, arithmetic and copies ran while one was open for 2% of the time, Pallas kernels for 0%

profile of v1, /device:TPU:1, one launch (start us, length us, event | category | flops | bytes accessed | tf_op | source)
XLA Modules:
  0.0 139.8 jit_solution(8503348394787570184)
XLA Ops:
  0.0 0.8 maximum_reduce_fusion
  0.8 33.6 %all_to_all.20 = bf16[32,24,128]{2,1,0:T(8,128)(2,1)S(1)} all-to-all(bf16[32,24,128]{2,1,0:T(8,128)(2,1)S(1)} %broadcast_in_dim.22), channel_id=1, replica_groups=mesh['y'=4,'xh'=2,'z'=16,'xl'=2,'c'=2] {'z','xl'}, dimensions={0} | all-to-all | bytes 393216 | tf_op jit(solution)/shard_map/all_to_all | solution.py:197
  34.4 5.0 %all_gather.6.q_ref = bf16[64,24,128]{2,1,0:T(8,128)(2,1)S(1)} all-gather(bf16[32,24,128]{2,1,0:T(8,128)(2,1)S(1)} %all_to_all.20), channel_id=1, replica_groups=mesh['y'=4,'xh'=2,'z'=16,'xl'=2,'c'=2] {'c'}, dimensions={0}, use_global_device_ids=true | all-gather | bytes 589824 | tf_op jit(solution)/shard_map/all_gather | solution.py:198
  39.4 1.4 %copy-done = f32[1792,224]{0,1:T(8,128)S(1)} copy-done((f32[1792,224]{0,1:T(8,128)S(1)}, f32[1792,224]{0,1:T(8,128)}, u32[]{:S(2)}) %copy-start) | copy-done | bytes 1605656
  40.8 1.0 copy-done.2
  41.8 0.7 shard_map.100
  42.6 0.0 copy-start.3
  42.6 0.9 broadcast_in_dim.23
  43.5 6.4 %all-to-all-start.1 = ((f32[8,64,384]{2,1,0:T(8,128)}), f32[8,64,384]{2,1,0:T(8,128)S(1)}, u32[]{:S(2)}, u32[]{:S(2)}) async-start(f32[8,64,384]{2,1,0:T(8,128)} %broadcast_in_dim.23), calls=%async_computation.1 | async-start | bytes 1572864 | tf_op jit(solution)/shard_map/all_to_all | solution.py:206
  49.9 0.7 constant_dynamic-slice_fusion.1
  51.8 0.8 add_divide_fusion.1
  52.6 0.8 add_divide_fusion
  53.4 0.1 pad_maximum_fusion
  53.4 10.0 %all-to-all-done.1.part_ref = f32[8,64,384]{2,1,0:T(8,128)S(1)} async-done(((f32[8,64,384]{2,1,0:T(8,128)}), f32[8,64,384]{2,1,0:T(8,128)S(1)}, u32[]{:S(2)}, u32[]{:S(2)}) %all-to-all-start.1) | async-done | bytes 786464 | tf_op jit(solution)/shard_map/all_to_all | solution.py:206
  63.4 0.8 shard_map.101
  64.2 3.7 %collective-permute-start = (f32[32,2816]{1,0:T(8,128)S(1)}, f32[32,2816]{1,0:T(8,128)S(1)}, u32[]{:S(2)}, u32[]{:S(2)}) collective-permute-start(f32[32,2816]{1,0:T(8,128)S(1)} %get-tuple-element.8), channel_id=1, source_target_pairs={{0,1},{1,0},{2,3},{3,2},{4,5},{5,4},{6,7},{7,6},{8,9},{9,8},{10,11... | collective-permute-start | bytes 1081352 | tf_op jit(solution)/shard_map/ppermute | solution.py:226
  68.0 1.3 collective-permute-done.got_ref
  69.3 0.2 shard_map.102
  69.5 21.8 %all_to_all.21.code_ref = s16[32,24,128]{2,1,0:T(8,128)(2,1)S(1)} all-to-all(s16[32,24,128]{2,1,0:T(8,128)(2,1)S(1)} %shard_map.102), channel_id=1, replica_groups=mesh['y'=4,'xh'=2,'z'=16,'xl'=2,'c'=2] {'z','xl'}, dimensions={0} | all-to-all | bytes 393216 | tf_op jit(solution)/shard_map/all_to_all | solution.py:233
  91.2 0.9 shard_map.103
  92.2 3.5 %all-to-all-start.3 = ((s16[16,24,128]{2,1,0:T(8,128)(2,1)}), s16[16,24,128]{2,1,0:T(8,128)(2,1)S(1)}, u32[]{:S(2)}, u32[]{:S(2)}) async-start(s16[16,24,128]{2,1,0:T(8,128)(2,1)} %shard_map.103), calls=%async_computation.3 | async-start | bytes 196608 | tf_op jit(solution)/shard_map/all_to_all | solution.py:238
  96.3 11.1 %all-to-all-done.3 = s16[16,24,128]{2,1,0:T(8,128)(2,1)S(1)} async-done(((s16[16,24,128]{2,1,0:T(8,128)(2,1)}), s16[16,24,128]{2,1,0:T(8,128)(2,1)S(1)}, u32[]{:S(2)}, u32[]{:S(2)}) %all-to-all-start.3) | async-done | bytes 98336 | tf_op jit(solution)/shard_map/all_to_all | solution.py:238
  107.4 27.9 %all-gather.1.code_ref = s16[512,24,128]{2,1,0:T(8,128)(2,1)S(1)} all-gather(s16[16,24,128]{2,1,0:T(8,128)(2,1)S(1)} %all-to-all-done.3), channel_id=1, replica_groups=mesh['y'=4,'xh'=2,'z'=16,'xl'=2,'c'=2] {'y','xh','xl','c'}, dimensions={0}, use_global_device_ids=true | all-gather | bytes 3244032 | tf_op jit(solution)/shard_map/all_gather | solution.py:239
  135.4 4.4 %shard_map.104 = f32[2,2]{1,0:T(2,128)} custom-call(s32[1]{0:T(128)S(6)} %copy.11.live_ref, s16[512,24,128]{2,1,0:T(8,128)(2,1)S(1)} %all-gather.1.code_ref, bf16[64,14336]{1,0:T(8,128)(2,1)S(1)} %copy-done.4, bf16[64,8192]{1,0:T(8,128)(2,1)S(1)} %copy-done.5), custom_call_target="tpu_custom_call" | custom-call | tf_op jit(solution)/shard_map/pallas_call | solution.py:240
  (15 shorter events, 0.1 us)
Async XLA Ops:
  39.4 1.4 %copy-start = (f32[1792,224]{0,1:T(8,128)S(1)}, f32[1792,224]{0,1:T(8,128)}, u32[]{:S(2)}) copy-start(f32[1792,224]{0,1:T(8,128)} %param.12) | copy-start | bytes 4816900
  40.8 1.0 copy-start.2
  42.6 7.3 %copy-start.6 = (s32[2,64]{1,0:T(2,128)S(1)}, s32[2,64]{1,0:T(2,128)}, u32[]{:S(2)}) copy-start(s32[2,64]{1,0:T(2,128)} %param.16) | copy-start | bytes 1540
  42.6 20.9 %copy-start.1 = (f32[1792,224]{0,1:T(8,128)S(1)}, f32[1792,224]{0,1:T(8,128)}, u32[]{:S(2)}) copy-start(f32[1792,224]{0,1:T(8,128)} %param.12) | copy-start | bytes 4816900
  42.6 20.9 %copy-start.3 = (f32[1024,128]{1,0:T(8,128)S(1)}, f32[1024,128]{1,0:T(8,128)}, u32[]{:S(2)}) copy-start(f32[1024,128]{1,0:T(8,128)} %bi_ref.3) | copy-start | bytes 1572868
  43.5 19.9 %all-to-all-start.1 = ((f32[8,64,384]{2,1,0:T(8,128)}), f32[8,64,384]{2,1,0:T(8,128)S(1)}, u32[]{:S(2)}, u32[]{:S(2)}) async-start(f32[8,64,384]{2,1,0:T(8,128)} %broadcast_in_dim.23), calls=%async_computation.1 | async-start | bytes 1572864 | tf_op jit(solution)/shard_map/all_to_all | solution.py:206
  64.2 5.0 %collective-permute-start = (f32[32,2816]{1,0:T(8,128)S(1)}, f32[32,2816]{1,0:T(8,128)S(1)}, u32[]{:S(2)}, u32[]{:S(2)}) collective-permute-start(f32[32,2816]{1,0:T(8,128)S(1)} %get-tuple-element.8), channel_id=1, source_target_pairs={{0,1},{1,0},{2,3},{3,2},{4,5},{5,4},{6,7},{7,6},{8,9},{9,8},{10,11... | collective-permute-start | bytes 1081352 | tf_op jit(solution)/shard_map/ppermute | solution.py:226
  91.2 44.1 %copy-start.4 = (bf16[64,14336]{1,0:T(8,128)(2,1)S(1)}, bf16[64,14336]{1,0:T(8,128)(2,1)}, u32[]{:S(2)}) copy-start(bf16[64,14336]{1,0:T(8,128)(2,1)} %to_ref.1) | copy-start | bytes 5505028
  91.2 44.1 %copy-start.5 = (bf16[64,8192]{1,0:T(8,128)(2,1)S(1)}, bf16[64,8192]{1,0:T(8,128)(2,1)}, u32[]{:S(2)}) copy-start(bf16[64,8192]{1,0:T(8,128)(2,1)} %ti_ref.1) | copy-start | bytes 3145732
  92.2 15.3 %all-to-all-start.3 = ((s16[16,24,128]{2,1,0:T(8,128)(2,1)}), s16[16,24,128]{2,1,0:T(8,128)(2,1)S(1)}, u32[]{:S(2)}, u32[]{:S(2)}) async-start(s16[16,24,128]{2,1,0:T(8,128)(2,1)} %shard_map.103), calls=%async_computation.3 | async-start | bytes 196608 | tf_op jit(solution)/shard_map/all_to_all | solution.py:238

commit v2 on v1

v2 whole, which is shorter than its diff:
```python
import functools

import jax
import jax.numpy as jnp
from jax import lax
from jax.experimental import pallas as pl
from jax.experimental.pallas import tpu as pltpu
from jax.sharding import Mesh
from jax.sharding import PartitionSpec as P

NQ = 2
SEQ_DEV = 2
RANK = 32
DAMPING = 0.5
LANES = 128
SLOTS = 24
STEPS = 8
TOP = 32766.0
OWN_FLOPS = 20_000_000_000
PAD = 32
GRP = ("y", "xh")
BLK = ("z", "xl", "c")
VMEM_LIMIT = 12 * 1024 * 1024

f32 = jnp.float32
bf16 = jnp.bfloat16


def split2(x):
    hi = x.astype(bf16)
    return hi, (x - hi.astype(f32)).astype(bf16)


def dot_nn(a, b):
    return lax.dot_general(a, b, (((1,), (0,)), ((), ())), preferred_element_type=f32)


def dot_nt(a, b):
    return lax.dot_general(a, b, (((1,), (1,)), ((), ())), preferred_element_type=f32)


def call(body, out_shape, scratch=(), n_in=1, smem=(), flops=0):
    specs = [
        pl.BlockSpec(memory_space=pltpu.SMEM if i in smem else pltpu.VMEM) for i in range(n_in)
    ]
    outs = jax.tree.map(lambda _: pl.BlockSpec(memory_space=pltpu.VMEM), out_shape)
    return pl.pallas_call(
        body,
        out_shape=out_shape,
        in_specs=specs,
        out_specs=outs,
        scratch_shapes=list(scratch),
        cost_estimate=pl.CostEstimate(flops=flops, bytes_accessed=0, transcendentals=0)
        if flops
        else None,
        compiler_params=pltpu.CompilerParams(vmem_limit_bytes=VMEM_LIMIT),
    )


def level(top):
    return jnp.ceil(STEPS * jnp.log2(jnp.maximum(top, 1e-30)))


def unit(steps):
    return jnp.exp2(steps * (1.0 / STEPS)) * (1.0 / TOP)


def to_code(x):
    return x.astype(jnp.int32).astype(jnp.int16)


def from_code(x):
    return x.astype(jnp.int32).astype(f32)


def split_body(bto_ref, bi_ref, out_ref):
    w_out, k_out = bto_ref.shape
    k_in = bi_ref.shape[0]
    rest = jnp.zeros((out_ref.shape[1] - w_out, k_out - k_in), bf16)
    for part, (b_out, b_in) in enumerate(zip(split2(bto_ref[...]), split2(bi_ref[...].T))):
        out_ref[part, :w_out, :] = b_out
        out_ref[part, w_out:, :k_in] = b_in
        out_ref[part, w_out:, k_in:] = rest


def rotate(rows, b_ref, w_out, k_out, k_in):
    n = rows.shape[0]
    w_pad = w_out + PAD
    lane = lax.broadcasted_iota(jnp.int32, (n, w_pad), 1)
    q_out, q_in = rows[:, :k_out], rows[:, k_out:]
    out = dot_nt(q_out, b_ref[0, :w_pad, :]) + dot_nt(q_out, b_ref[1, :w_pad, :])
    out = jnp.where(lane < w_out, out, 0.0)
    inn = dot_nt(q_in, b_ref[0, w_out:, :k_in]) + dot_nt(q_in, b_ref[1, w_out:, :k_in])
    s_out = level(jnp.max(jnp.abs(out), axis=1, keepdims=True))
    s_in = level(jnp.max(jnp.abs(inn), axis=1, keepdims=True))
    out = jnp.round(out * (1.0 / unit(s_out)))
    out = jnp.where(lane < w_out, out, jnp.where(lane < w_out + PAD // 2, s_out, s_in))
    inn = jnp.round(inn * (1.0 / unit(s_in)))
    return to_code(out), to_code(inn)


def rotate_own_body(n_out, n_in, w_out, q_ref, b_ref, rows_ref, code_ref, wide):
    n = q_ref.shape[0]
    wide[...] = q_ref[...].astype(f32).reshape(wide.shape)
    for r in range(n_out + n_in):
        rows_ref[:, r * LANES : (r + 1) * LANES] = wide[pl.ds(r, n, stride=SLOTS), :].astype(bf16)
    out, inn = rotate(rows_ref, b_ref, w_out, n_out * LANES, n_in * LANES)
    code_ref[:, : w_out + PAD] = out
    code_ref[:, w_out + PAD :] = inn


def rotate_mate_body(n_out, n_in, w_out, rows_ref, b_ref, code_ref, part_ref):
    out, inn = rotate(rows_ref, b_ref, w_out, n_out * LANES, n_in * LANES)
    w_all = code_ref.shape[1]
    for g in range(part_ref.shape[0]):
        part_ref[g, :, :w_all] = code_ref[...]
        part_ref[g, :, w_all : w_all + w_out + PAD] = out
        part_ref[g, :, w_all + w_out + PAD :] = inn


def panel_scales(spot, w_out, panel_ref, eo_ref, ei_ref):
    start = panel_ref[0, spot] * w_out
    row, shift = start // LANES, start % LANES
    last = eo_ref.shape[0] - 1
    spans = -(-w_out // LANES) + 1
    held = jnp.concatenate(
        [eo_ref[pl.ds(jnp.minimum(row + i, last), 1), :] for i in range(spans)], axis=1
    )
    picked = held[:, : w_out + PAD]
    for by in range(PAD, LANES, PAD):
        picked = jnp.where(shift == by, held[:, by : by + w_out + PAD], picked)
    e_in = ei_ref[pl.ds(panel_ref[1, spot], 1), :]
    return 1.0 / (picked + DAMPING), 1.0 / (e_in + DAMPING)


def restore_body(
    n_out, n_in, w_out, at_ref, panel_ref, part_ref, eo_ref, ei_ref, own_ref, mate_ref, code_ref, wide
):
    n = part_ref.shape[1]
    k_out, k_in = n_out * LANES, n_in * LANES
    w_in = own_ref.shape[1] - w_out
    w_pad = w_out + PAD
    w_all = w_pad + w_in
    lane = lax.broadcasted_iota(jnp.int32, (n, w_pad), 1)
    x_out = jnp.zeros((n, k_out), f32)
    x_in = jnp.zeros((n, k_in), f32)
    for k, b_ref in enumerate((own_ref, mate_ref)):
        at = k * w_all
        t_out = jnp.zeros((n, w_pad), f32)
        t_in = jnp.zeros((n, w_in), f32)
        for g in range(part_ref.shape[0]):
            x = from_code(part_ref[g, :, at : at + w_all])
            t_out += x[:, :w_pad] * unit(x[:, w_out : w_out + 1])
            t_in += x[:, w_pad:] * unit(x[:, w_out + PAD // 2 : w_out + PAD // 2 + 1])
        s_out, s_in = panel_scales(at_ref[k], w_out, panel_ref, eo_ref, ei_ref)
        t_out = jnp.where(lane < w_out, t_out * s_out, 0.0)
        both = jnp.concatenate(split2(t_out), axis=0)
        x = dot_nn(both, b_ref[0, :w_pad, :])
        x_out += x[:n] + x[n:] + dot_nn(both[:n], b_ref[1, :w_pad, :])
        both = jnp.concatenate(split2(t_in * s_in), axis=0)
        x = dot_nn(both, b_ref[0, w_out:, :k_in])
        x_in += x[:n] + x[n:] + dot_nn(both[:n], b_ref[1, w_out:, :k_in])
    for first, x, row in ((0, x_out, n_out + n_in), (n_out, x_in, n_out + n_in + 1)):
        steps = level(jnp.max(jnp.abs(x), axis=1, keepdims=True))
        codes = jnp.round(x * (1.0 / unit(steps)))
        for r in range(x.shape[1] // LANES):
            wide[pl.ds(first + r, n, stride=SLOTS), :] = codes[:, r * LANES : (r + 1) * LANES]
        wide[pl.ds(row, n, stride=SLOTS), :] = jnp.broadcast_to(steps, (n, LANES))
    code_ref[...] = to_code(wide[...]).reshape(code_ref.shape)


def sum_codes_body(n_out, n_in, code_ref, out_ref):
    slot = lax.broadcasted_iota(jnp.int32, (SLOTS, LANES), 0)
    is_out = slot < n_out
    is_in = jnp.logical_and(slot >= n_out, slot < n_out + n_in)
    total = jnp.zeros((SLOTS, LANES), f32)
    for j in range(code_ref.shape[0]):
        x = from_code(code_ref[j])
        a = x[n_out + n_in : n_out + n_in + 1]
        b = x[n_out + n_in + 1 : n_out + n_in + 2]
        total = total + x * unit(jnp.where(is_out, a, b))
    size = jnp.abs(total)
    steps_out = level(jnp.max(jnp.where(is_out, size, 0.0), keepdims=True))
    steps_in = level(jnp.max(jnp.where(is_in, size, 0.0), keepdims=True))
    steps = jnp.where(is_out, steps_out, steps_in)
    codes = jnp.round(total * (1.0 / unit(steps)))
    codes = jnp.where(slot == n_out + n_in, steps_out, codes)
    codes = jnp.where(slot == n_out + n_in + 1, steps_in, codes)
    codes = to_code(codes)
    for j in range(out_ref.shape[0]):
        out_ref[j] = codes


def score_body(n_out, n_in, groups, live_ref, code_ref, to_ref, ti_ref, out_ref, wide, hi, lo):
    n = code_ref.shape[0] // groups
    along_out = jnp.zeros((to_ref.shape[0], n), f32)
    along_in = jnp.zeros((ti_ref.shape[0], n), f32)
    for g in range(groups):
        x = from_code(code_ref[g * n : (g + 1) * n])
        wide[...] = x.reshape(wide.shape)
        for first, count, row in ((0, n_out, n_out + n_in), (n_out, n_in, n_out + n_in + 1)):
            scale = unit(wide[pl.ds(row, n, stride=SLOTS), :])
            for r in range(count):
                v = wide[pl.ds(first + r, n, stride=SLOTS), :] * scale
                a, b = split2(v)
                hi[:, r * LANES : (r + 1) * LANES] = a
                lo[:, r * LANES : (r + 1) * LANES] = b
            width = count * LANES
            t_ref = to_ref if first == 0 else ti_ref
            t = t_ref[:, g * width : (g + 1) * width]
            part = dot_nt(t, hi[:, :width]) + dot_nt(t, lo[:, :width])
            if first == 0:
                along_out = along_out + part
            else:
                along_in = along_in + part
    product = along_out * along_in
    rows = product.shape[0]
    q_id = lax.rem(lax.broadcasted_iota(jnp.int32, (rows, n), 1), 16) // 8
    s_id = lax.broadcasted_iota(jnp.int32, (rows, n), 0) // RANK
    row = lax.broadcasted_iota(jnp.int32, out_ref.shape, 0)
    col = lax.broadcasted_iota(jnp.int32, out_ref.shape, 1)
    result = jnp.zeros(out_ref.shape, f32)
    for s in range(SEQ_DEV):
        for q in range(NQ):
            picked = jnp.where(jnp.logical_and(s_id == s, q_id == q), product, 0.0)
            value = jnp.sum(picked) * (1.0 / RANK)
            value = jnp.where(live_ref[0] > s, value, 0.0)
            result = jnp.where(jnp.logical_and(row == s, col == q), value, result)
    out_ref[...] = result


def spread(x, axes):
    n = lax.axis_size(axes)
    x = jnp.broadcast_to(x[None], (n, *x.shape))
    return lax.all_to_all(x, axes, split_axis=0, concat_axis=0, tiled=True)


def per_device(qo, qi, bo, bi, eo, ei, panels, to, ti, live):
    n_out, n_in = qo.shape[1] // LANES, qi.shape[1] // LANES
    data = n_out + n_in
    nz, nxl, nc = (lax.axis_size(a) for a in BLK)
    n_grp = lax.axis_size(GRP)
    half = nz * nxl
    n_rows = half * nc
    position = lax.axis_index(BLK)
    w_out, w_in = bo.shape[1], bi.shape[1]
    w_all = w_out + PAD + w_in

    own_q = jnp.concatenate([qo, qi], axis=1).reshape(data, LANES)
    own_q = jnp.pad(own_q, ((0, SLOTS - data), (0, 0)))
    queries = spread(own_q, ("z", "xl"))

    own = call(
        split_body, jax.ShapeDtypeStruct((2, w_out + w_in, bo.shape[0]), bf16), n_in=2
    )(bo.T, bi)
    mate = lax.ppermute(own, "c", [(0, 1), (1, 0)])
    rows, own_part = call(
        functools.partial(rotate_own_body, n_out, n_in, w_out),
        (
            jax.ShapeDtypeStruct((half, data * LANES), bf16),
            jax.ShapeDtypeStruct((half, w_all), jnp.int16),
        ),
        [pltpu.VMEM((half * SLOTS, LANES), f32)],
        n_in=2,
        flops=OWN_FLOPS,
    )(queries, own)
    part = call(
        functools.partial(rotate_mate_body, n_out, n_in, w_out),
        jax.ShapeDtypeStruct((n_grp, half, nc * w_all), jnp.int16),
        n_in=3,
    )(rows, mate, own_part)
    parts = lax.all_to_all(part, GRP, split_axis=0, concat_axis=0, tiled=True)

    mate_spot = position + 1 - 2 * lax.axis_index("c")
    spots = jnp.stack([position, mate_spot]).astype(jnp.int32)
    codes = call(
        functools.partial(restore_body, n_out, n_in, w_out),
        jax.ShapeDtypeStruct((half, SLOTS, LANES), jnp.int16),
        [pltpu.VMEM((half * SLOTS, LANES), f32)],
        n_in=7,
        smem=(0, 1),
    )(spots, panels, parts, eo.reshape(-1, LANES), ei.reshape(-1, w_in), own, mate)
    codes = lax.all_to_all(codes, ("z", "xl"), split_axis=0, concat_axis=0, tiled=True)
    codes = call(
        functools.partial(sum_codes_body, n_out, n_in),
        jax.ShapeDtypeStruct((nz, SLOTS, LANES), jnp.int16),
    )(codes)
    codes = lax.all_to_all(codes, "z", split_axis=0, concat_axis=0, tiled=True)
    codes = lax.all_gather(codes, ("y", "xh", "xl", "c"), axis=0, tiled=True)
    return call(
        functools.partial(score_body, n_out, n_in, n_grp),
        jax.ShapeDtypeStruct((SEQ_DEV, NQ), f32),
        [
            pltpu.VMEM((n_rows * SLOTS, LANES), f32),
            pltpu.VMEM((n_rows, n_out * LANES), bf16),
            pltpu.VMEM((n_rows, n_out * LANES), bf16),
        ],
        n_in=4,
        smem=(0,),
    )(live, codes, to, ti)


def solution(mesh):
    fine = Mesh(mesh.devices.reshape(4, 2, 16, 2, 2), GRP + BLK)
    in_specs = (
        P(BLK, GRP),
        P(BLK, GRP),
        P(GRP, BLK),
        P(GRP, BLK),
        P(),
        P(),
        P(),
        P(GRP + BLK, None),
        P(GRP + BLK, None),
        P(GRP + BLK),
    )
    out_specs = P(GRP + BLK, None)
    return jax.shard_map(
        per_device, mesh=fine, in_specs=in_specs, out_specs=out_specs, check_vma=False
    )
```

time: 140 us -> 131 us (0.936)
  blocking collectives: 88.3 us -> 51.8 us
  starting transfers between devices: 13.6 us -> 29.9 us
  waiting for transfers between devices: 22.4 us -> 30.4 us
  Pallas kernels: 7.09 us -> 13.3 us
  other arithmetic: 2.38 us -> 0.83 us
    all_to_all x1 -> x0, blocking collectives: 33.6 us -> none  [per_device(): lax.all_to_all(spread, ('z', 'xl'), split_axis=0, concat_axis=0, tiled=True)]
    all_to_all x1 -> x2, starting transfers between devices: 6.36 us -> 23.3 us  [the longest x1 17 us: spread(): return lax.all_to_all(x, axes, split_axis=0, concat_axis=0, tiled=True)]
    all_to_all x1 -> x2, waiting for transfers between devices: 9.99 us -> 19.2 us  [the longest x1 10.9 us: spread(): return lax.all_to_all(x, axes, split_axis=0, concat_axis=0, tiled=True)]
    pallas_call x3 -> x4, Pallas kernels: 1.73 us -> 7.93 us  [the longest x1 3.4 us: per_device(): call(functools.partial(rotate_mate_body, n_out, n_in, w_out), jax.ShapeDt...]
    all_gather x1 -> x0, blocking collectives: 4.96 us -> none  [per_device(): queries = lax.all_gather(got, 'c', axis=0, tiled=True)]
    all_gather x1, blocking collectives: 27.9 us -> 30.6 us  [per_device(): codes = lax.all_gather(codes, ('y', 'xh', 'xl', 'c'), axis=0, tiled=True)]
    div x2 -> x0, other arithmetic: 1.55 us -> none  [panel_scale(): return 1.0 / (picked + DAMPING)]
  transfers between devices with their start and end apart: 3 -> 4, of which waited for: 3 -> 3; matrix products, arithmetic and copies ran while one was open for 2% -> 0% of each run, Pallas kernels for 0% -> 1%
where the time goes in v2:
time: 131 us; the launch traced here: 130 us
  blocking collectives  51.8 us (40%)
  waiting for transfers between devices  30.4 us (23%)
  starting transfers between devices  29.9 us (23%)
  Pallas kernels  13.3 us (10%)
  local copies, waits for them, and re-layouts  3.2 us (2%)
    all_gather x1, blocking collectives, per_device(): codes = lax.all_gather(codes, ('y', 'xh', 'xl', 'c'), axis=0, tiled=True)  30.6 us
    all_to_all x1, blocking collectives, per_device(): lax.all_to_all(codes, ('z', 'xl'), split_axis=0, concat_axis=0, tiled=True)  21.1 us
    all_to_all x1, starting transfers between devices, spread(): return lax.all_to_all(x, axes, split_axis=0, concat_axis=0, tiled=True)  17 us
    all_to_all x1, waiting for transfers between devices, per_device(): codes = lax.all_to_all(codes, 'z', split_axis=0, concat_axis=0, tiled=True)  11.2 us
    all_to_all x1, waiting for transfers between devices, spread(): return lax.all_to_all(x, axes, split_axis=0, concat_axis=0, tiled=True)  10.9 us
    all_to_all x1, waiting for transfers between devices, per_device(): parts = lax.all_to_all(part, GRP, split_axis=0, concat_axis=0, tiled=True)  8.32 us
    all_to_all x1, starting transfers between devices, per_device(): parts = lax.all_to_all(part, GRP, split_axis=0, concat_axis=0, tiled=True)  6.36 us
    pallas_call x1, Pallas kernels, per_device(): call(functools.partial(score_body, n_out, n_in, n_grp), jax.ShapeDtypeStr...  4.44 us
  transfers between devices with their start and end apart: 4, of which 3 were waited for; matrix products, arithmetic and copies ran while one was open for 0% of the time, Pallas kernels for 1%

profile of v2, /device:TPU:1, one launch (start us, length us, event | category | flops | bytes accessed | tf_op | source)
XLA Modules:
  0.0 130.1 jit_solution(3549741719057341941)
XLA Ops:
  0.0 0.8 maximum_reduce_fusion
  0.8 0.7 broadcast_in_dim.2
  1.5 17.0 %all-to-all-start = ((bf16[32,24,128]{2,1,0:T(8,128)(2,1)}), bf16[32,24,128]{2,1,0:T(8,128)(2,1)S(1)}, u32[]{:S(2)}, u32[]{:S(2)}) async-start(bf16[32,24,128]{2,1,0:T(8,128)(2,1)} %broadcast_in_dim.2), calls=%async_computation | async-start | bytes 393216 | tf_op jit(solution)/shard_map/all_to_all | solution.py:235
  18.4 0.0 copy-start.1
  18.5 1.4 %copy-done.1 = f32[1792,224]{0,1:T(8,128)S(1)} copy-done((f32[1792,224]{0,1:T(8,128)S(1)}, f32[1792,224]{0,1:T(8,128)}, u32[]{:S(2)}) %copy-start.1) | copy-done | bytes 1605656
  19.9 1.0 copy-done.3
  20.9 0.6 shard_map.100.b_ref.own_ref
  21.5 2.9 %collective-permute-start = (bf16[2,352,1792]{2,1,0:T(8,128)(2,1)S(1)}, bf16[2,352,1792]{2,1,0:T(8,128)(2,1)}, u32[]{:S(2)}, u32[]{:S(2)}) collective-permute-start(bf16[2,352,1792]{2,1,0:T(8,128)(2,1)S(1)} %shard_map.100.b_ref.own_ref), channel_id=1, source_target_pairs={{0,1},{1,0},{2,3},{3,2},{4,5},{5,4},{6,7},{7,6},{8,9},{9,8},{10,11... | collective-permute-start | bytes 7569416 | tf_op jit(solution)/shard_map/ppermute | solution.py:256
  24.4 10.9 %all-to-all-done.q_ref = bf16[32,24,128]{2,1,0:T(8,128)(2,1)S(1)} async-done(((bf16[32,24,128]{2,1,0:T(8,128)(2,1)}), bf16[32,24,128]{2,1,0:T(8,128)(2,1)S(1)}, u32[]{:S(2)}, u32[]{:S(2)}) %all-to-all-start) | async-done | bytes 196640 | tf_op jit(solution)/shard_map/all_to_all | solution.py:235
  35.3 0.9 shard_map.101
  36.2 0.0 copy-start.5
  36.3 0.0 copy-start.6
  36.3 3.4 %shard_map.102 = s16[8,32,768]{2,1,0:T(8,128)(2,1)} custom-call(bf16[32,2816]{1,0:T(8,128)(2,1)S(1)} %get-tuple-element.7.rows_ref, bf16[2,352,1792]{2,1,0:T(8,128)(2,1)} %collective-permute-done.b_ref.mate_ref, s16[32,384]{1,0:T(8,128)(2,1)S(1)} %get-tuple-element.8.code_ref), custom_call_target="tpu_custom_call" | custom-call | tf_op jit(solution)/shard_map/pallas_call | solution.py:267
  39.7 6.4 %all-to-all-start.1 = ((s16[8,32,768]{2,1,0:T(8,128)(2,1)}), s16[8,32,768]{2,1,0:T(8,128)(2,1)S(1)}, u32[]{:S(2)}, u32[]{:S(2)}) async-start(s16[8,32,768]{2,1,0:T(8,128)(2,1)} %shard_map.102), calls=%async_computation.1 | async-start | bytes 786432 | tf_op jit(solution)/shard_map/all_to_all | solution.py:272
  46.0 0.1 pad_add_fusion.at_ref
  46.1 8.3 %all-to-all-done.1.part_ref = s16[8,32,768]{2,1,0:T(8,128)(2,1)S(1)} async-done(((s16[8,32,768]{2,1,0:T(8,128)(2,1)}), s16[8,32,768]{2,1,0:T(8,128)(2,1)S(1)}, u32[]{:S(2)}, u32[]{:S(2)}) %all-to-all-start.1) | async-done | bytes 393248 | tf_op jit(solution)/shard_map/all_to_all | solution.py:272
  54.4 3.0 %shard_map.103 = s16[32,24,128]{2,1,0:T(8,128)(2,1)S(1)} custom-call(s32[2]{0:T(128)S(1)} %pad_add_fusion.at_ref, s32[2,64]{1,0:T(2,128)S(1)} %copy-done.6, s16[8,32,768]{2,1,0:T(8,128)(2,1)S(1)} %all-to-all-done.1.part_ref, f32[112,128]{1,0:T(8,128)S(1)} %bitcast.7, f32[64,128]{1,0:T(8,128)S(1)} %bitcast.8, ...), custom_call_target="tpu_custom_call" | custom-call | tf_op jit(solution)/shard_map/pallas_call | solution.py:276
  57.5 0.0 copy-start
  57.5 21.1 %all_to_all.20.code_ref = s16[32,24,128]{2,1,0:T(8,128)(2,1)S(1)} all-to-all(s16[32,24,128]{2,1,0:T(8,128)(2,1)S(1)} %shard_map.103), channel_id=1, replica_groups=mesh['y'=4,'xh'=2,'z'=16,'xl'=2,'c'=2] {'z','xl'}, dimensions={0} | all-to-all | bytes 393216 | tf_op jit(solution)/shard_map/all_to_all | solution.py:283
  78.6 0.9 shard_map.104
  79.5 3.7 %all-to-all-start.3 = ((s16[16,24,128]{2,1,0:T(8,128)(2,1)}), s16[16,24,128]{2,1,0:T(8,128)(2,1)S(1)}, u32[]{:S(2)}, u32[]{:S(2)}) async-start(s16[16,24,128]{2,1,0:T(8,128)(2,1)} %shard_map.104), calls=%async_computation.3 | async-start | bytes 196608 | tf_op jit(solution)/shard_map/all_to_all | solution.py:288
  83.9 11.2 %all-to-all-done.3 = s16[16,24,128]{2,1,0:T(8,128)(2,1)S(1)} async-done(((s16[16,24,128]{2,1,0:T(8,128)(2,1)}), s16[16,24,128]{2,1,0:T(8,128)(2,1)S(1)}, u32[]{:S(2)}, u32[]{:S(2)}) %all-to-all-start.3) | async-done | bytes 98336 | tf_op jit(solution)/shard_map/all_to_all | solution.py:288
  95.1 30.6 %all-gather.1.code_ref = s16[512,24,128]{2,1,0:T(8,128)(2,1)S(1)} all-gather(s16[16,24,128]{2,1,0:T(8,128)(2,1)S(1)} %all-to-all-done.3), channel_id=1, replica_groups=mesh['y'=4,'xh'=2,'z'=16,'xl'=2,'c'=2] {'y','xh','xl','c'}, dimensions={0}, use_global_device_ids=true | all-gather | bytes 3244032 | tf_op jit(solution)/shard_map/all_gather | solution.py:289
  125.7 4.4 %shard_map.105 = f32[2,2]{1,0:T(2,128)} custom-call(s32[1]{0:T(128)S(6)} %copy.11.live_ref, s16[512,24,128]{2,1,0:T(8,128)(2,1)S(1)} %all-gather.1.code_ref, bf16[64,14336]{1,0:T(8,128)(2,1)S(1)} %copy-done, bf16[64,8192]{1,0:T(8,128)(2,1)S(1)} %copy-done.2), custom_call_target="tpu_custom_call" | custom-call | tf_op jit(solution)/shard_map/pallas_call | solution.py:290
  (10 shorter events, 0.0 us)
Async XLA Ops:
  1.5 33.8 %all-to-all-start = ((bf16[32,24,128]{2,1,0:T(8,128)(2,1)}), bf16[32,24,128]{2,1,0:T(8,128)(2,1)S(1)}, u32[]{:S(2)}, u32[]{:S(2)}) async-start(bf16[32,24,128]{2,1,0:T(8,128)(2,1)} %broadcast_in_dim.2), calls=%async_computation | async-start | bytes 393216 | tf_op jit(solution)/shard_map/all_to_all | solution.py:235
  18.4 1.4 %copy-start.1 = (f32[1792,224]{0,1:T(8,128)S(1)}, f32[1792,224]{0,1:T(8,128)}, u32[]{:S(2)}) copy-start(f32[1792,224]{0,1:T(8,128)} %param.12) | copy-start | bytes 4816900
  19.9 1.0 copy-start.3
  21.5 14.8 %collective-permute-start = (bf16[2,352,1792]{2,1,0:T(8,128)(2,1)S(1)}, bf16[2,352,1792]{2,1,0:T(8,128)(2,1)}, u32[]{:S(2)}, u32[]{:S(2)}) collective-permute-start(bf16[2,352,1792]{2,1,0:T(8,128)(2,1)S(1)} %shard_map.100.b_ref.own_ref), channel_id=1, source_target_pairs={{0,1},{1,0},{2,3},{3,2},{4,5},{5,4},{6,7},{7,6},{8,9},{9,8},{10,11... | collective-permute-start | bytes 7569416 | tf_op jit(solution)/shard_map/ppermute | solution.py:256
  36.2 18.2 %copy-start.4 = (f32[14336]{0:T(1024)S(1)}, f32[14336]{0:T(1024)}, u32[]{:S(2)}) copy-start(f32[14336]{0:T(1024)} %param.14) | copy-start | bytes 172036
  36.2 18.2 %copy-start.5 = (f32[8192]{0:T(1024)S(1)}, f32[8192]{0:T(1024)}, u32[]{:S(2)}) copy-start(f32[8192]{0:T(1024)} %param.15) | copy-start | bytes 98308
  36.3 18.2 %copy-start.6 = (s32[2,64]{1,0:T(2,128)S(1)}, s32[2,64]{1,0:T(2,128)}, u32[]{:S(2)}) copy-start(s32[2,64]{1,0:T(2,128)} %panel_ref.1) | copy-start | bytes 1540
  39.7 14.8 %all-to-all-start.1 = ((s16[8,32,768]{2,1,0:T(8,128)(2,1)}), s16[8,32,768]{2,1,0:T(8,128)(2,1)S(1)}, u32[]{:S(2)}, u32[]{:S(2)}) async-start(s16[8,32,768]{2,1,0:T(8,128)(2,1)} %shard_map.102), calls=%async_computation.1 | async-start | bytes 786432 | tf_op jit(solution)/shard_map/all_to_all | solution.py:272
  57.5 68.2 %copy-start = (bf16[64,14336]{1,0:T(8,128)(2,1)S(1)}, bf16[64,14336]{1,0:T(8,128)(2,1)}, u32[]{:S(2)}) copy-start(bf16[64,14336]{1,0:T(8,128)(2,1)} %to_ref.1) | copy-start | bytes 5505028
  57.5 68.2 %copy-start.2 = (bf16[64,8192]{1,0:T(8,128)(2,1)S(1)}, bf16[64,8192]{1,0:T(8,128)(2,1)}, u32[]{:S(2)}) copy-start(bf16[64,8192]{1,0:T(8,128)(2,1)} %ti_ref.1) | copy-start | bytes 3145732
  79.5 15.5 %all-to-all-start.3 = ((s16[16,24,128]{2,1,0:T(8,128)(2,1)}), s16[16,24,128]{2,1,0:T(8,128)(2,1)S(1)}, u32[]{:S(2)}, u32[]{:S(2)}) async-start(s16[16,24,128]{2,1,0:T(8,128)(2,1)} %shard_map.104), calls=%async_computation.3 | async-start | bytes 196608 | tf_op jit(solution)/shard_map/all_to_all | solution.py:288

commit v3 on v2

--- a/solution.py
+++ b/solution.py
@@ -73,6 +73,21 @@
     return x.astype(jnp.int32).astype(f32)
 
 
+def panel_scales(spot, w_out, panel_ref, eo_ref, ei_ref):
+    start = panel_ref[0, spot] * w_out
+    row, shift = start // LANES, start % LANES
+    last = eo_ref.shape[0] - 1
+    spans = -(-w_out // LANES) + 1
+    held = jnp.concatenate(
+        [eo_ref[pl.ds(jnp.minimum(row + i, last), 1), :] for i in range(spans)], axis=1
+    )
+    picked = held[:, : w_out + PAD]
+    for by in range(PAD, LANES, PAD):
+        picked = jnp.where(shift == by, held[:, by : by + w_out + PAD], picked)
+    e_in = ei_ref[pl.ds(panel_ref[1, spot], 1), :]
+    return 1.0 / (picked + DAMPING), 1.0 / (e_in + DAMPING)
+
+
 def split_body(bto_ref, bi_ref, out_ref):
     w_out, k_out = bto_ref.shape
     k_in = bi_ref.shape[0]
@@ -99,7 +114,30 @@
     return to_code(out), to_code(inn)
 
 
-def rotate_own_body(n_out, n_in, w_out, q_ref, b_ref, rows_ref, code_ref, wide):
+def rotate_own_body(
+    n_out,
+    n_in,
+    w_out,
+    at_ref,
+    panel_ref,
+    live_ref,
+    eo_ref,
+    ei_ref,
+    q_ref,
+    b_ref,
+    rows_ref,
+    code_ref,
+    scale_ref,
+    count_ref,
+    wide,
+):
+    count_ref[...] = jnp.full(count_ref.shape, live_ref[0], jnp.int32)
+    w_pad = w_out + PAD
+    w_all = scale_ref.shape[1] // 2
+    for k in range(2):
+        s_out, s_in = panel_scales(at_ref[k], w_out, panel_ref, eo_ref, ei_ref)
+        scale_ref[:, k * w_all : k * w_all + w_pad] = s_out
+        scale_ref[:, k * w_all + w_pad : (k + 1) * w_all] = s_in
     n = q_ref.shape[0]
     wide[...] = q_ref[...].astype(f32).reshape(wide.shape)
     for r in range(n_out + n_in):
@@ -118,24 +156,7 @@
         part_ref[g, :, w_all + w_out + PAD :] = inn
 
 
-def panel_scales(spot, w_out, panel_ref, eo_ref, ei_ref):
-    start = panel_ref[0, spot] * w_out
-    row, shift = start // LANES, start % LANES
-    last = eo_ref.shape[0] - 1
-    spans = -(-w_out // LANES) + 1
-    held = jnp.concatenate(
-        [eo_ref[pl.ds(jnp.minimum(row + i, last), 1), :] for i in range(spans)], axis=1
-    )
-    picked = held[:, : w_out + PAD]
-    for by in range(PAD, LANES, PAD):
-        picked = jnp.where(shift == by, held[:, by : by + w_out + PAD], picked)
-    e_in = ei_ref[pl.ds(panel_ref[1, spot], 1), :]
-    return 1.0 / (picked + DAMPING), 1.0 / (e_in + DAMPING)
-
-
-def restore_body(
-    n_out, n_in, w_out, at_ref, panel_ref, part_ref, eo_ref, ei_ref, own_ref, mate_ref, code_ref, wide
-):
+def restore_body(n_out, n_in, w_out, part_ref, scale_ref, own_ref, mate_ref, code_ref, wide):
     n = part_ref.shape[1]
     k_out, k_in = n_out * LANES, n_in * LANES
     w_in = own_ref.shape[1] - w_out
@@ -152,12 +173,12 @@
             x = from_code(part_ref[g, :, at : at + w_all])
             t_out += x[:, :w_pad] * unit(x[:, w_out : w_out + 1])
             t_in += x[:, w_pad:] * unit(x[:, w_out + PAD // 2 : w_out + PAD // 2 + 1])
-        s_out, s_in = panel_scales(at_ref[k], w_out, panel_ref, eo_ref, ei_ref)
-        t_out = jnp.where(lane < w_out, t_out * s_out, 0.0)
+        t_out = jnp.where(lane < w_out, t_out * scale_ref[:, at : at + w_pad], 0.0)
+        t_in = t_in * scale_ref[:, at + w_pad : at + w_all]
         both = jnp.concatenate(split2(t_out), axis=0)
         x = dot_nn(both, b_ref[0, :w_pad, :])
         x_out += x[:n] + x[n:] + dot_nn(both[:n], b_ref[1, :w_pad, :])
-        both = jnp.concatenate(split2(t_in * s_in), axis=0)
+        both = jnp.concatenate(split2(t_in), axis=0)
         x = dot_nn(both, b_ref[0, w_out:, :k_in])
         x_in += x[:n] + x[n:] + dot_nn(both[:n], b_ref[1, w_out:, :k_in])
     for first, x, row in ((0, x_out, n_out + n_in), (n_out, x_in, n_out + n_in + 1)):
@@ -191,42 +212,45 @@
         out_ref[j] = codes
 
 
-def score_body(n_out, n_in, groups, live_ref, code_ref, to_ref, ti_ref, out_ref, wide, hi, lo):
+def score_body(n_out, n_in, groups, count_ref, code_ref, to_ref, ti_ref, out_ref, wide, both):
     n = code_ref.shape[0] // groups
-    along_out = jnp.zeros((to_ref.shape[0], n), f32)
-    along_in = jnp.zeros((ti_ref.shape[0], n), f32)
+    rows = to_ref.shape[0]
+    k_out = n_out * LANES
+    along_out = jnp.zeros((2 * n, rows), f32)
+    along_in = jnp.zeros((2 * n, rows), f32)
     for g in range(groups):
         x = from_code(code_ref[g * n : (g + 1) * n])
         wide[...] = x.reshape(wide.shape)
         for first, count, row in ((0, n_out, n_out + n_in), (n_out, n_in, n_out + n_in + 1)):
             scale = unit(wide[pl.ds(row, n, stride=SLOTS), :])
-            for r in range(count):
-                v = wide[pl.ds(first + r, n, stride=SLOTS), :] * scale
-                a, b = split2(v)
-                hi[:, r * LANES : (r + 1) * LANES] = a
-                lo[:, r * LANES : (r + 1) * LANES] = b
+            for r in range(first, first + count):
+                hi, lo = split2(wide[pl.ds(r, n, stride=SLOTS), :] * scale)
+                both[:n, r * LANES : (r + 1) * LANES] = hi
+                both[n:, r * LANES : (r + 1) * LANES] = lo
             width = count * LANES
-            t_ref = to_ref if first == 0 else ti_ref
-            t = t_ref[:, g * width : (g + 1) * width]
-            part = dot_nt(t, hi[:, :width]) + dot_nt(t, lo[:, :width])
+            part = both[:, first * LANES : (first + count) * LANES]
             if first == 0:
-                along_out = along_out + part
+                along_out += dot_nt(part, to_ref[:, g * width : (g + 1) * width])
             else:
-                along_in = along_in + part
-    product = along_out * along_in
-    rows = product.shape[0]
-    q_id = lax.rem(lax.broadcasted_iota(jnp.int32, (rows, n), 1), 16) // 8
-    s_id = lax.broadcasted_iota(jnp.int32, (rows, n), 0) // RANK
+                along_in += dot_nt(part, ti_ref[:, g * width : (g + 1) * width])
+    product = (along_out[:n] + along_out[n:]) * (along_in[:n] + along_in[n:])
+    span = 16 // NQ
+    by_query = []
+    for q in range(NQ):
+        total = product[q * span : (q + 1) * span]
+        for first in range((q + NQ) * span, n, NQ * span):
+            total = total + product[first : first + span]
+        by_query.append(jnp.sum(total, axis=0, keepdims=True))
+    s_id = lax.broadcasted_iota(jnp.int32, (1, rows), 1) // RANK
     row = lax.broadcasted_iota(jnp.int32, out_ref.shape, 0)
     col = lax.broadcasted_iota(jnp.int32, out_ref.shape, 1)
     result = jnp.zeros(out_ref.shape, f32)
     for s in range(SEQ_DEV):
         for q in range(NQ):
-            picked = jnp.where(jnp.logical_and(s_id == s, q_id == q), product, 0.0)
-            value = jnp.sum(picked) * (1.0 / RANK)
-            value = jnp.where(live_ref[0] > s, value, 0.0)
+            picked = jnp.where(s_id == s, by_query[q], 0.0)
+            value = jnp.sum(picked, axis=1, keepdims=True) * (1.0 / RANK)
             result = jnp.where(jnp.logical_and(row == s, col == q), value, result)
-    out_ref[...] = result
+    out_ref[...] = jnp.where(row < count_ref[:, :NQ], result, 0.0)
 
 
 def spread(x, axes):
@@ -250,20 +274,25 @@
     own_q = jnp.pad(own_q, ((0, SLOTS - data), (0, 0)))
     queries = spread(own_q, ("z", "xl"))
 
+    mate_spot = position + 1 - 2 * lax.axis_index("c")
+    spots = jnp.stack([position, mate_spot]).astype(jnp.int32)
     own = call(
         split_body, jax.ShapeDtypeStruct((2, w_out + w_in, bo.shape[0]), bf16), n_in=2
     )(bo.T, bi)
     mate = lax.ppermute(own, "c", [(0, 1), (1, 0)])
-    rows, own_part = call(
+    rows, own_part, scale, count = call(
         functools.partial(rotate_own_body, n_out, n_in, w_out),
         (
             jax.ShapeDtypeStruct((half, data * LANES), bf16),
             jax.ShapeDtypeStruct((half, w_all), jnp.int16),
+            jax.ShapeDtypeStruct((1, nc * w_all), f32),
+            jax.ShapeDtypeStruct((SEQ_DEV, LANES), jnp.int32),
         ),
         [pltpu.VMEM((half * SLOTS, LANES), f32)],
-        n_in=2,
+        n_in=7,
+        smem=(0, 1, 2),
         flops=OWN_FLOPS,
-    )(queries, own)
+    )(spots, panels, live, eo.reshape(-1, LANES), ei.reshape(-1, w_in), queries, own)
     part = call(
         functools.partial(rotate_mate_body, n_out, n_in, w_out),
         jax.ShapeDtypeStruct((n_grp, half, nc * w_all), jnp.int16),
@@ -271,15 +300,12 @@
     )(rows, mate, own_part)
     parts = lax.all_to_all(part, GRP, split_axis=0, concat_axis=0, tiled=True)
 
-    mate_spot = position + 1 - 2 * lax.axis_index("c")
-    spots = jnp.stack([position, mate_spot]).astype(jnp.int32)
     codes = call(
         functools.partial(restore_body, n_out, n_in, w_out),
         jax.ShapeDtypeStruct((half, SLOTS, LANES), jnp.int16),
         [pltpu.VMEM((half * SLOTS, LANES), f32)],
-        n_in=7,
-        smem=(0, 1),
-    )(spots, panels, parts, eo.reshape(-1, LANES), ei.reshape(-1, w_in), own, mate)
+        n_in=4,
+    )(parts, scale, own, mate)
     codes = lax.all_to_all(codes, ("z", "xl"), split_axis=0, concat_axis=0, tiled=True)
     codes = call(
         functools.partial(sum_codes_body, n_out, n_in),
@@ -292,12 +318,10 @@
         jax.ShapeDtypeStruct((SEQ_DEV, NQ), f32),
         [
             pltpu.VMEM((n_rows * SLOTS, LANES), f32),
-            pltpu.VMEM((n_rows, n_out * LANES), bf16),
-            pltpu.VMEM((n_rows, n_out * LANES), bf16),
+            pltpu.VMEM((2 * n_rows, data * LANES), bf16),
         ],
         n_in=4,
-        smem=(0,),
-    )(live, codes, to, ti)
+    )(count, codes, to, ti)
 
 
 def solution(mesh):

time: 131 us -> 128 us (0.977)
  blocking collectives: 51.8 us -> 80.6 us
  waiting for transfers between devices: 30.4 us -> 10.2 us
  starting transfers between devices: 29.9 us -> 20 us
    all_to_all x0 -> x2, blocking collectives: none -> 29.9 us  [the longest x1 15.2 us: per_device(): codes = lax.all_to_all(codes, 'z', split_axis=0, concat_axis=0, tiled=True)]
    all_to_all x2 -> x0, waiting for transfers between devices: 19.5 us -> none  [the longest x1 11.2 us: per_device(): codes = lax.all_to_all(codes, 'z', split_axis=0, concat_axis=0, tiled=True)]
    all_to_all x2 -> x0, starting transfers between devices: 10.1 us -> none  [the longest x1 6.36 us: per_device(): parts = lax.all_to_all(part, GRP, split_axis=0, concat_axis=0, tiled=True)]
  transfers between devices with their start and end apart: 4 -> 2, of which waited for: 3 -> 1; matrix products, arithmetic and copies ran while one was open for 0% -> 0% of each run, Pallas kernels for 1% -> 2%
where the time goes in v3:
time: 128 us
  blocking collectives  80.6 us (63%)
  starting transfers between devices  20 us (16%)
  Pallas kernels  12.2 us (10%)
  waiting for transfers between devices  10.2 us (8%)
  local copies, waits for them, and re-layouts  3.21 us (3%)
    all_gather x1, blocking collectives, per_device(): codes = lax.all_gather(codes, ('y', 'xh', 'xl', 'c'), axis=0, tiled=True)  30.5 us
    all_to_all x1, blocking collectives, per_device(): lax.all_to_all(codes, ('z', 'xl'), split_axis=0, concat_axis=0, tiled=True)  20.2 us
    all_to_all x1, starting transfers between devices, spread(): return lax.all_to_all(x, axes, split_axis=0, concat_axis=0, tiled=True)  17.1 us
    all_to_all x1, blocking collectives, per_device(): codes = lax.all_to_all(codes, 'z', split_axis=0, concat_axis=0, tiled=True)  15.2 us
    all_to_all x1, blocking collectives, per_device(): parts = lax.all_to_all(part, GRP, split_axis=0, concat_axis=0, tiled=True)  14.7 us
    all_to_all x1, waiting for transfers between devices, spread(): return lax.all_to_all(x, axes, split_axis=0, concat_axis=0, tiled=True)  10.2 us
    pallas_call x1, Pallas kernels, per_device(): call(functools.partial(score_body, n_out, n_in, n_grp), jax.ShapeDtypeStr...  4.41 us
    ppermute x1, starting transfers between devices, per_device(): mate = lax.ppermute(own, 'c', [(0, 1), (1, 0)])  2.86 us
  transfers between devices with their start and end apart: 2, of which 1 were waited for; matrix products, arithmetic and copies ran while one was open for 0% of the time, Pallas kernels for 2%

profile of v3, /device:TPU:1, one launch (start us, length us, event | category | flops | bytes accessed | tf_op | source)
XLA Modules:
  0.0 127.7 jit_solution(6923698032895980087)
XLA Ops:
  0.0 0.8 maximum_reduce_fusion
  0.8 0.7 broadcast_in_dim.2
  1.5 17.1 %all-to-all-start = ((bf16[32,24,128]{2,1,0:T(8,128)(2,1)}), bf16[32,24,128]{2,1,0:T(8,128)(2,1)S(1)}, u32[]{:S(2)}, u32[]{:S(2)}) async-start(bf16[32,24,128]{2,1,0:T(8,128)(2,1)} %broadcast_in_dim.2), calls=%async_computation | async-start | bytes 393216 | tf_op jit(solution)/shard_map/all_to_all | solution.py:259
  18.6 0.0 copy-start.1
  18.6 1.4 %copy-done.1 = f32[1792,224]{0,1:T(8,128)S(1)} copy-done((f32[1792,224]{0,1:T(8,128)S(1)}, f32[1792,224]{0,1:T(8,128)}, u32[]{:S(2)}) %copy-start.1) | copy-done | bytes 1605656
  20.0 1.0 copy-done.3
  21.1 0.6 shard_map.100.b_ref.own_ref
  21.7 2.9 %collective-permute-start = (bf16[2,352,1792]{2,1,0:T(8,128)(2,1)S(1)}, bf16[2,352,1792]{2,1,0:T(8,128)(2,1)}, u32[]{:S(2)}, u32[]{:S(2)}) collective-permute-start(bf16[2,352,1792]{2,1,0:T(8,128)(2,1)S(1)} %shard_map.100.b_ref.own_ref), channel_id=1, source_target_pairs={{0,1},{1,0},{2,3},{3,2},{4,5},{5,4},{6,7},{7,6},{8,9},{9,8},{10,11... | collective-permute-start | bytes 7569416 | tf_op jit(solution)/shard_map/ppermute | solution.py:282
  25.2 0.1 pad_add_fusion.at_ref
  25.3 10.2 %all-to-all-done.q_ref = bf16[32,24,128]{2,1,0:T(8,128)(2,1)S(1)} async-done(((bf16[32,24,128]{2,1,0:T(8,128)(2,1)}), bf16[32,24,128]{2,1,0:T(8,128)(2,1)S(1)}, u32[]{:S(2)}, u32[]{:S(2)}) %all-to-all-start) | async-done | bytes 196640 | tf_op jit(solution)/shard_map/all_to_all | solution.py:259
  35.5 0.0 copy-done.5
  35.5 1.5 %shard_map.101 = (bf16[32,2816]{1,0:T(8,128)(2,1)S(1)}, s16[32,384]{1,0:T(8,128)(2,1)S(1)}, f32[1,768]{1,0:T(1,128)S(1)}, s32[2,128]{1,0:T(2,128)S(1)}) custom-call(s32[2]{0:T(128)S(1)} %pad_add_fusion.at_ref, s32[2,64]{1,0:T(2,128)S(1)} %copy-done.6, s32[1]{0:T(128)S(6)} %copy.11.live_ref, f32[112,128]{1,0:T(8,128)S(1)} %bitcast.7, f32[64,128]{1,0:T(8,128)S(1)} %bitcast.8, ...), custom_call_target="tpu_custom_call" | custom-call | flops 20000000000 | tf_op jit(solution)/shard_map/pallas_call | solution.py:283
  37.0 0.0 collective-permute-done.b_ref.mate_ref
  37.0 2.6 %shard_map.102 = s16[8,32,768]{2,1,0:T(8,128)(2,1)S(1)} custom-call(bf16[32,2816]{1,0:T(8,128)(2,1)S(1)} %get-tuple-element.10.rows_ref, bf16[2,352,1792]{2,1,0:T(8,128)(2,1)} %collective-permute-done.b_ref.mate_ref, s16[32,384]{1,0:T(8,128)(2,1)S(1)} %get-tuple-element.11.code_ref), custom_call_target="tpu_custom_call" | custom-call | tf_op jit(solution)/shard_map/pallas_call | solution.py:296
  39.6 14.7 %all_to_all.20.part_ref = s16[8,32,768]{2,1,0:T(8,128)(2,1)S(1)} all-to-all(s16[8,32,768]{2,1,0:T(8,128)(2,1)S(1)} %shard_map.102), channel_id=1, replica_groups=mesh['y'=4,'xh'=2,'z'=16,'xl'=2,'c'=2] {'y','xh'}, dimensions={0} | all-to-all | bytes 786432 | tf_op jit(solution)/shard_map/all_to_all | solution.py:301
  54.3 2.8 %shard_map.103 = s16[32,24,128]{2,1,0:T(8,128)(2,1)S(1)} custom-call(s16[8,32,768]{2,1,0:T(8,128)(2,1)S(1)} %all_to_all.20.part_ref, f32[1,768]{1,0:T(1,128)S(1)} %get-tuple-element.12.scale_ref, bf16[2,352,1792]{2,1,0:T(8,128)(2,1)S(1)} %shard_map.100.b_ref.own_ref, bf16[2,352,1792]{2,1,0:T(8,128)(2,1)} %collective-permute-done.b_ref.mate_ref), custom_call_target="tpu_custom_call" | custom-call | tf_op jit(solution)/shard_map/pallas_call | solution.py:303
  57.1 0.0 copy-start
  57.1 0.0 copy-start.2
  57.1 20.2 %all_to_all.21.code_ref = s16[32,24,128]{2,1,0:T(8,128)(2,1)S(1)} all-to-all(s16[32,24,128]{2,1,0:T(8,128)(2,1)S(1)} %shard_map.103), channel_id=1, replica_groups=mesh['y'=4,'xh'=2,'z'=16,'xl'=2,'c'=2] {'z','xl'}, dimensions={0} | all-to-all | bytes 393216 | tf_op jit(solution)/shard_map/all_to_all | solution.py:309
  77.3 0.3 shard_map.104
  77.6 15.2 %all_to_all.22 = s16[16,24,128]{2,1,0:T(8,128)(2,1)S(1)} all-to-all(s16[16,24,128]{2,1,0:T(8,128)(2,1)S(1)} %shard_map.104), channel_id=1, replica_groups=mesh['y'=4,'xh'=2,'z'=16,'xl'=2,'c'=2] {'z'}, dimensions={0} | all-to-all | bytes 196608 | tf_op jit(solution)/shard_map/all_to_all | solution.py:314
  92.8 30.5 %all-gather.1.code_ref = s16[512,24,128]{2,1,0:T(8,128)(2,1)S(1)} all-gather(s16[16,24,128]{2,1,0:T(8,128)(2,1)S(1)} %all_to_all.22), channel_id=1, replica_groups=mesh['y'=4,'xh'=2,'z'=16,'xl'=2,'c'=2] {'y','xh','xl','c'}, dimensions={0}, use_global_device_ids=true | all-gather | bytes 3244032 | tf_op jit(solution)/shard_map/all_gather | solution.py:315
  123.3 0.0 copy-done
  123.3 4.4 %shard_map.105 = f32[2,2]{1,0:T(2,128)} custom-call(s32[2,128]{1,0:T(2,128)S(1)} %get-tuple-element.9.count_ref, s16[512,24,128]{2,1,0:T(8,128)(2,1)S(1)} %all-gather.1.code_ref, bf16[64,14336]{1,0:T(8,128)(2,1)S(1)} %copy-done, bf16[64,8192]{1,0:T(8,128)(2,1)S(1)} %copy-done.2), custom_call_target="tpu_custom_call" | custom-call | tf_op jit(solution)/shard_map/pallas_call | solution.py:316
  (8 shorter events, 0.0 us)
Async XLA Ops:
  1.5 34.0 %copy-start.4 = (f32[14336]{0:T(1024)S(1)}, f32[14336]{0:T(1024)}, u32[]{:S(2)}) copy-start(f32[14336]{0:T(1024)} %param.14) | copy-start | bytes 172036
  1.5 34.0 %copy-start.5 = (f32[8192]{0:T(1024)S(1)}, f32[8192]{0:T(1024)}, u32[]{:S(2)}) copy-start(f32[8192]{0:T(1024)} %param.15) | copy-start | bytes 98308
  1.5 34.0 %copy-start.6 = (s32[2,64]{1,0:T(2,128)S(1)}, s32[2,64]{1,0:T(2,128)}, u32[]{:S(2)}) copy-start(s32[2,64]{1,0:T(2,128)} %panel_ref.1) | copy-start | bytes 1540
  1.5 34.0 %all-to-all-start = ((bf16[32,24,128]{2,1,0:T(8,128)(2,1)}), bf16[32,24,128]{2,1,0:T(8,128)(2,1)S(1)}, u32[]{:S(2)}, u32[]{:S(2)}) async-start(bf16[32,24,128]{2,1,0:T(8,128)(2,1)} %broadcast_in_dim.2), calls=%async_computation | async-start | bytes 393216 | tf_op jit(solution)/shard_map/all_to_all | solution.py:259
  18.6 1.4 %copy-start.1 = (f32[1792,224]{0,1:T(8,128)S(1)}, f32[1792,224]{0,1:T(8,128)}, u32[]{:S(2)}) copy-start(f32[1792,224]{0,1:T(8,128)} %param.12) | copy-start | bytes 4816900
  20.0 1.0 copy-start.3
  21.7 15.3 %collective-permute-start = (bf16[2,352,1792]{2,1,0:T(8,128)(2,1)S(1)}, bf16[2,352,1792]{2,1,0:T(8,128)(2,1)}, u32[]{:S(2)}, u32[]{:S(2)}) collective-permute-start(bf16[2,352,1792]{2,1,0:T(8,128)(2,1)S(1)} %shard_map.100.b_ref.own_ref), channel_id=1, source_target_pairs={{0,1},{1,0},{2,3},{3,2},{4,5},{5,4},{6,7},{7,6},{8,9},{9,8},{10,11... | collective-permute-start | bytes 7569416 | tf_op jit(solution)/shard_map/ppermute | solution.py:282
  57.1 66.2 %copy-start = (bf16[64,14336]{1,0:T(8,128)(2,1)S(1)}, bf16[64,14336]{1,0:T(8,128)(2,1)}, u32[]{:S(2)}) copy-start(bf16[64,14336]{1,0:T(8,128)(2,1)} %to_ref.1) | copy-start | bytes 5505028
  57.1 66.1 %copy-start.2 = (bf16[64,8192]{1,0:T(8,128)(2,1)S(1)}, bf16[64,8192]{1,0:T(8,128)(2,1)}, u32[]{:S(2)}) copy-start(bf16[64,8192]{1,0:T(8,128)(2,1)} %ti_ref.1) | copy-start | bytes 3145732

commit v4 on v3

--- a/solution.py
+++ b/solution.py
@@ -212,27 +212,26 @@
         out_ref[j] = codes
 
 
-def score_body(n_out, n_in, groups, count_ref, code_ref, to_ref, ti_ref, out_ref, wide, both):
+def score_body(n_out, n_in, groups, count_ref, code_ref, to_ref, ti_ref, out_ref, wide):
     n = code_ref.shape[0] // groups
     rows = to_ref.shape[0]
-    k_out = n_out * LANES
-    along_out = jnp.zeros((2 * n, rows), f32)
-    along_in = jnp.zeros((2 * n, rows), f32)
+    alongs = [jnp.zeros((2 * n, rows), f32)] * 2
+    sides = ((0, n_out, to_ref), (n_out, n_in, ti_ref))
     for g in range(groups):
-        x = from_code(code_ref[g * n : (g + 1) * n])
-        wide[...] = x.reshape(wide.shape)
-        for first, count, row in ((0, n_out, n_out + n_in), (n_out, n_in, n_out + n_in + 1)):
-            scale = unit(wide[pl.ds(row, n, stride=SLOTS), :])
-            for r in range(first, first + count):
-                hi, lo = split2(wide[pl.ds(r, n, stride=SLOTS), :] * scale)
-                both[:n, r * LANES : (r + 1) * LANES] = hi
-                both[n:, r * LANES : (r + 1) * LANES] = lo
-            width = count * LANES
-            part = both[:, first * LANES : (first + count) * LANES]
-            if first == 0:
-                along_out += dot_nt(part, to_ref[:, g * width : (g + 1) * width])
-            else:
-                along_in += dot_nt(part, ti_ref[:, g * width : (g + 1) * width])
+        wide[...] = from_code(code_ref[g * n : (g + 1) * n]).reshape(wide.shape)
+
+        def row(r):
+            return wide[pl.ds(r, n, stride=SLOTS), :]
+
+        for side, (first, count, t_ref) in enumerate(sides):
+            scale = unit(row(n_out + n_in + side))
+            scale = jnp.concatenate([scale, scale], axis=1)
+            for r in range(0, count, 2):
+                pair = jnp.concatenate([row(first + r), row(first + r + 1)], axis=1)
+                both = jnp.concatenate(split2(pair * scale), axis=0)
+                at = (g * count + r) * LANES
+                alongs[side] += dot_nt(both, t_ref[:, at : at + 2 * LANES])
+    along_out, along_in = alongs
     product = (along_out[:n] + along_out[n:]) * (along_in[:n] + along_in[n:])
     span = 16 // NQ
     by_query = []
@@ -318,7 +317,6 @@
         jax.ShapeDtypeStruct((SEQ_DEV, NQ), f32),
         [
             pltpu.VMEM((n_rows * SLOTS, LANES), f32),
-            pltpu.VMEM((2 * n_rows, data * LANES), bf16),
         ],
         n_in=4,
     )(count, codes, to, ti)

time: 128 us -> 127 us (level)
  no operation moved by 1% of the time
where the time goes in v4:
time: 127 us
  blocking collectives  80.6 us (63%)
  starting transfers between devices  20 us (16%)
  Pallas kernels  11.4 us (9%)
  waiting for transfers between devices  10.2 us (8%)
  local copies, waits for them, and re-layouts  3.21 us (3%)
    all_gather x1, blocking collectives, per_device(): codes = lax.all_gather(codes, ('y', 'xh', 'xl', 'c'), axis=0, tiled=True)  30.5 us
    all_to_all x1, blocking collectives, per_device(): lax.all_to_all(codes, ('z', 'xl'), split_axis=0, concat_axis=0, tiled=True)  20.2 us
    all_to_all x1, starting transfers between devices, spread(): return lax.all_to_all(x, axes, split_axis=0, concat_axis=0, tiled=True)  17.1 us
    all_to_all x1, blocking collectives, per_device(): codes = lax.all_to_all(codes, 'z', split_axis=0, concat_axis=0, tiled=True)  15.2 us
    all_to_all x1, blocking collectives, per_device(): parts = lax.all_to_all(part, GRP, split_axis=0, concat_axis=0, tiled=True)  14.7 us
    all_to_all x1, waiting for transfers between devices, spread(): return lax.all_to_all(x, axes, split_axis=0, concat_axis=0, tiled=True)  10.2 us
    pallas_call x1, Pallas kernels, per_device(): call(functools.partial(score_body, n_out, n_in, n_grp), jax.ShapeDtypeStr...  3.62 us
    ppermute x1, starting transfers between devices, per_device(): mate = lax.ppermute(own, 'c', [(0, 1), (1, 0)])  2.86 us
  transfers between devices with their start and end apart: 2, of which 1 were waited for; matrix products, arithmetic and copies ran while one was open for 0% of the time, Pallas kernels for 2%

profile of v4, /device:TPU:1, one launch (start us, length us, event | category | flops | bytes accessed | tf_op | source)
XLA Modules:
  0.0 126.9 jit_solution(1764771371636514523)
XLA Ops:
  0.0 0.8 maximum_reduce_fusion
  0.8 0.7 broadcast_in_dim.2
  1.5 17.1 %all-to-all-start = ((bf16[32,24,128]{2,1,0:T(8,128)(2,1)}), bf16[32,24,128]{2,1,0:T(8,128)(2,1)S(1)}, u32[]{:S(2)}, u32[]{:S(2)}) async-start(bf16[32,24,128]{2,1,0:T(8,128)(2,1)} %broadcast_in_dim.2), calls=%async_computation | async-start | bytes 393216 | tf_op jit(solution)/shard_map/all_to_all | solution.py:258
  18.6 0.0 copy-start.1
  18.6 1.4 %copy-done.1 = f32[1792,224]{0,1:T(8,128)S(1)} copy-done((f32[1792,224]{0,1:T(8,128)S(1)}, f32[1792,224]{0,1:T(8,128)}, u32[]{:S(2)}) %copy-start.1) | copy-done | bytes 1605656
  20.0 1.0 copy-done.3
  21.1 0.6 shard_map.100.b_ref.own_ref
  21.7 2.9 %collective-permute-start = (bf16[2,352,1792]{2,1,0:T(8,128)(2,1)S(1)}, bf16[2,352,1792]{2,1,0:T(8,128)(2,1)}, u32[]{:S(2)}, u32[]{:S(2)}) collective-permute-start(bf16[2,352,1792]{2,1,0:T(8,128)(2,1)S(1)} %shard_map.100.b_ref.own_ref), channel_id=1, source_target_pairs={{0,1},{1,0},{2,3},{3,2},{4,5},{5,4},{6,7},{7,6},{8,9},{9,8},{10,11... | collective-permute-start | bytes 7569416 | tf_op jit(solution)/shard_map/ppermute | solution.py:281
  25.2 0.1 pad_add_fusion.at_ref
  25.3 10.2 %all-to-all-done.q_ref = bf16[32,24,128]{2,1,0:T(8,128)(2,1)S(1)} async-done(((bf16[32,24,128]{2,1,0:T(8,128)(2,1)}), bf16[32,24,128]{2,1,0:T(8,128)(2,1)S(1)}, u32[]{:S(2)}, u32[]{:S(2)}) %all-to-all-start) | async-done | bytes 196640 | tf_op jit(solution)/shard_map/all_to_all | solution.py:258
  35.5 0.0 copy-done.5
  35.5 1.5 %shard_map.101 = (bf16[32,2816]{1,0:T(8,128)(2,1)S(1)}, s16[32,384]{1,0:T(8,128)(2,1)S(1)}, f32[1,768]{1,0:T(1,128)S(1)}, s32[2,128]{1,0:T(2,128)S(1)}) custom-call(s32[2]{0:T(128)S(1)} %pad_add_fusion.at_ref, s32[2,64]{1,0:T(2,128)S(1)} %copy-done.6, s32[1]{0:T(128)S(6)} %copy.11.live_ref, f32[112,128]{1,0:T(8,128)S(1)} %bitcast.7, f32[64,128]{1,0:T(8,128)S(1)} %bitcast.8, ...), custom_call_target="tpu_custom_call" | custom-call | flops 20000000000 | tf_op jit(solution)/shard_map/pallas_call | solution.py:282
  37.0 0.0 collective-permute-done.b_ref.mate_ref
  37.0 2.6 %shard_map.102 = s16[8,32,768]{2,1,0:T(8,128)(2,1)S(1)} custom-call(bf16[32,2816]{1,0:T(8,128)(2,1)S(1)} %get-tuple-element.10.rows_ref, bf16[2,352,1792]{2,1,0:T(8,128)(2,1)} %collective-permute-done.b_ref.mate_ref, s16[32,384]{1,0:T(8,128)(2,1)S(1)} %get-tuple-element.11.code_ref), custom_call_target="tpu_custom_call" | custom-call | tf_op jit(solution)/shard_map/pallas_call | solution.py:295
  39.6 14.7 %all_to_all.20.part_ref = s16[8,32,768]{2,1,0:T(8,128)(2,1)S(1)} all-to-all(s16[8,32,768]{2,1,0:T(8,128)(2,1)S(1)} %shard_map.102), channel_id=1, replica_groups=mesh['y'=4,'xh'=2,'z'=16,'xl'=2,'c'=2] {'y','xh'}, dimensions={0} | all-to-all | bytes 786432 | tf_op jit(solution)/shard_map/all_to_all | solution.py:300
  54.3 2.8 %shard_map.103 = s16[32,24,128]{2,1,0:T(8,128)(2,1)S(1)} custom-call(s16[8,32,768]{2,1,0:T(8,128)(2,1)S(1)} %all_to_all.20.part_ref, f32[1,768]{1,0:T(1,128)S(1)} %get-tuple-element.12.scale_ref, bf16[2,352,1792]{2,1,0:T(8,128)(2,1)S(1)} %shard_map.100.b_ref.own_ref, bf16[2,352,1792]{2,1,0:T(8,128)(2,1)} %collective-permute-done.b_ref.mate_ref), custom_call_target="tpu_custom_call" | custom-call | tf_op jit(solution)/shard_map/pallas_call | solution.py:302
  57.1 0.0 copy-start
  57.1 0.0 copy-start.2
  57.1 20.2 %all_to_all.21.code_ref = s16[32,24,128]{2,1,0:T(8,128)(2,1)S(1)} all-to-all(s16[32,24,128]{2,1,0:T(8,128)(2,1)S(1)} %shard_map.103), channel_id=1, replica_groups=mesh['y'=4,'xh'=2,'z'=16,'xl'=2,'c'=2] {'z','xl'}, dimensions={0} | all-to-all | bytes 393216 | tf_op jit(solution)/shard_map/all_to_all | solution.py:308
  77.3 0.3 shard_map.104
  77.6 15.2 %all_to_all.22 = s16[16,24,128]{2,1,0:T(8,128)(2,1)S(1)} all-to-all(s16[16,24,128]{2,1,0:T(8,128)(2,1)S(1)} %shard_map.104), channel_id=1, replica_groups=mesh['y'=4,'xh'=2,'z'=16,'xl'=2,'c'=2] {'z'}, dimensions={0} | all-to-all | bytes 196608 | tf_op jit(solution)/shard_map/all_to_all | solution.py:313
  92.8 30.5 %all-gather.1.code_ref = s16[512,24,128]{2,1,0:T(8,128)(2,1)S(1)} all-gather(s16[16,24,128]{2,1,0:T(8,128)(2,1)S(1)} %all_to_all.22), channel_id=1, replica_groups=mesh['y'=4,'xh'=2,'z'=16,'xl'=2,'c'=2] {'y','xh','xl','c'}, dimensions={0}, use_global_device_ids=true | all-gather | bytes 3244032 | tf_op jit(solution)/shard_map/all_gather | solution.py:314
  123.3 0.0 copy-done
  123.3 3.6 %shard_map.105 = f32[2,2]{1,0:T(2,128)} custom-call(s32[2,128]{1,0:T(2,128)S(1)} %get-tuple-element.9.count_ref, s16[512,24,128]{2,1,0:T(8,128)(2,1)S(1)} %all-gather.1.code_ref, bf16[64,14336]{1,0:T(8,128)(2,1)S(1)} %copy-done, bf16[64,8192]{1,0:T(8,128)(2,1)S(1)} %copy-done.2), custom_call_target="tpu_custom_call" | custom-call | tf_op jit(solution)/shard_map/pallas_call | solution.py:315
  (8 shorter events, 0.0 us)
Async XLA Ops:
  1.5 34.0 %copy-start.4 = (f32[14336]{0:T(1024)S(1)}, f32[14336]{0:T(1024)}, u32[]{:S(2)}) copy-start(f32[14336]{0:T(1024)} %param.14) | copy-start | bytes 172036
  1.5 34.0 %copy-start.5 = (f32[8192]{0:T(1024)S(1)}, f32[8192]{0:T(1024)}, u32[]{:S(2)}) copy-start(f32[8192]{0:T(1024)} %param.15) | copy-start | bytes 98308
  1.5 34.0 %copy-start.6 = (s32[2,64]{1,0:T(2,128)S(1)}, s32[2,64]{1,0:T(2,128)}, u32[]{:S(2)}) copy-start(s32[2,64]{1,0:T(2,128)} %panel_ref.1) | copy-start | bytes 1540
  1.5 34.0 %all-to-all-start = ((bf16[32,24,128]{2,1,0:T(8,128)(2,1)}), bf16[32,24,128]{2,1,0:T(8,128)(2,1)S(1)}, u32[]{:S(2)}, u32[]{:S(2)}) async-start(bf16[32,24,128]{2,1,0:T(8,128)(2,1)} %broadcast_in_dim.2), calls=%async_computation | async-start | bytes 393216 | tf_op jit(solution)/shard_map/all_to_all | solution.py:258
  18.6 1.4 %copy-start.1 = (f32[1792,224]{0,1:T(8,128)S(1)}, f32[1792,224]{0,1:T(8,128)}, u32[]{:S(2)}) copy-start(f32[1792,224]{0,1:T(8,128)} %param.12) | copy-start | bytes 4816900
  20.0 1.0 copy-start.3
  21.7 15.3 %collective-permute-start = (bf16[2,352,1792]{2,1,0:T(8,128)(2,1)S(1)}, bf16[2,352,1792]{2,1,0:T(8,128)(2,1)}, u32[]{:S(2)}, u32[]{:S(2)}) collective-permute-start(bf16[2,352,1792]{2,1,0:T(8,128)(2,1)S(1)} %shard_map.100.b_ref.own_ref), channel_id=1, source_target_pairs={{0,1},{1,0},{2,3},{3,2},{4,5},{5,4},{6,7},{7,6},{8,9},{9,8},{10,11... | collective-permute-start | bytes 7569416 | tf_op jit(solution)/shard_map/ppermute | solution.py:281
  57.1 66.2 %copy-start = (bf16[64,14336]{1,0:T(8,128)(2,1)S(1)}, bf16[64,14336]{1,0:T(8,128)(2,1)}, u32[]{:S(2)}) copy-start(bf16[64,14336]{1,0:T(8,128)(2,1)} %to_ref.1) | copy-start | bytes 5505028
  57.1 66.1 %copy-start.2 = (bf16[64,8192]{1,0:T(8,128)(2,1)S(1)}, bf16[64,8192]{1,0:T(8,128)(2,1)}, u32[]{:S(2)}) copy-start(bf16[64,8192]{1,0:T(8,128)(2,1)} %ti_ref.1) | copy-start | bytes 3145732

commit v5 on v4

--- a/solution.py
+++ b/solution.py
@@ -156,16 +156,22 @@
         part_ref[g, :, w_all + w_out + PAD :] = inn
 
 
-def restore_body(n_out, n_in, w_out, part_ref, scale_ref, own_ref, mate_ref, code_ref, wide):
+def back(both, b_hi, b_lo):
+    n = both.shape[0] // 2
+    x = dot_nn(both, b_hi)
+    return x[:n] + x[n:] + dot_nn(both[:n], b_lo)
+
+
+def restore_own_body(
+    n_out, n_in, w_out, part_ref, scale_ref, own_ref, x_ref, mate_out_ref, mate_in_ref
+):
     n = part_ref.shape[1]
     k_out, k_in = n_out * LANES, n_in * LANES
     w_in = own_ref.shape[1] - w_out
     w_pad = w_out + PAD
     w_all = w_pad + w_in
     lane = lax.broadcasted_iota(jnp.int32, (n, w_pad), 1)
-    x_out = jnp.zeros((n, k_out), f32)
-    x_in = jnp.zeros((n, k_in), f32)
-    for k, b_ref in enumerate((own_ref, mate_ref)):
+    for k in range(2):
         at = k * w_all
         t_out = jnp.zeros((n, w_pad), f32)
         t_in = jnp.zeros((n, w_in), f32)
@@ -175,12 +181,28 @@
             t_in += x[:, w_pad:] * unit(x[:, w_out + PAD // 2 : w_out + PAD // 2 + 1])
         t_out = jnp.where(lane < w_out, t_out * scale_ref[:, at : at + w_pad], 0.0)
         t_in = t_in * scale_ref[:, at + w_pad : at + w_all]
-        both = jnp.concatenate(split2(t_out), axis=0)
-        x = dot_nn(both, b_ref[0, :w_pad, :])
-        x_out += x[:n] + x[n:] + dot_nn(both[:n], b_ref[1, :w_pad, :])
-        both = jnp.concatenate(split2(t_in), axis=0)
-        x = dot_nn(both, b_ref[0, w_out:, :k_in])
-        x_in += x[:n] + x[n:] + dot_nn(both[:n], b_ref[1, w_out:, :k_in])
+        t_out = jnp.concatenate(split2(t_out), axis=0)
+        t_in = jnp.concatenate(split2(t_in), axis=0)
+        if k == 0:
+            x_ref[:, :k_out] = back(t_out, own_ref[0, :w_pad, :], own_ref[1, :w_pad, :])
+            x_ref[:, k_out:] = back(t_in, own_ref[0, w_out:, :k_in], own_ref[1, w_out:, :k_in])
+        else:
+            mate_out_ref[...] = t_out
+            mate_in_ref[...] = t_in
+
+
+def restore_mate_body(
+    n_out, n_in, w_out, x_ref, mate_out_ref, mate_in_ref, mate_ref, code_ref, wide
+):
+    n = x_ref.shape[0]
+    k_out, k_in = n_out * LANES, n_in * LANES
+    w_pad = w_out + PAD
+    x_out = x_ref[:, :k_out] + back(
+        mate_out_ref[...], mate_ref[0, :w_pad, :], mate_ref[1, :w_pad, :]
+    )
+    x_in = x_ref[:, k_out:] + back(
+        mate_in_ref[...], mate_ref[0, w_out:, :k_in], mate_ref[1, w_out:, :k_in]
+    )
     for first, x, row in ((0, x_out, n_out + n_in), (n_out, x_in, n_out + n_in + 1)):
         steps = level(jnp.max(jnp.abs(x), axis=1, keepdims=True))
         codes = jnp.round(x * (1.0 / unit(steps)))
@@ -299,12 +321,22 @@
     )(rows, mate, own_part)
     parts = lax.all_to_all(part, GRP, split_axis=0, concat_axis=0, tiled=True)
 
+    x_own, mate_out, mate_in = call(
+        functools.partial(restore_own_body, n_out, n_in, w_out),
+        (
+            jax.ShapeDtypeStruct((half, data * LANES), f32),
+            jax.ShapeDtypeStruct((2 * half, w_out + PAD), bf16),
+            jax.ShapeDtypeStruct((2 * half, w_in), bf16),
+        ),
+        n_in=3,
+        flops=OWN_FLOPS,
+    )(parts, scale, own)
     codes = call(
-        functools.partial(restore_body, n_out, n_in, w_out),
+        functools.partial(restore_mate_body, n_out, n_in, w_out),
         jax.ShapeDtypeStruct((half, SLOTS, LANES), jnp.int16),
         [pltpu.VMEM((half * SLOTS, LANES), f32)],
         n_in=4,
-    )(parts, scale, own, mate)
+    )(x_own, mate_out, mate_in, mate)
     codes = lax.all_to_all(codes, ("z", "xl"), split_axis=0, concat_axis=0, tiled=True)
     codes = call(
         functools.partial(sum_codes_body, n_out, n_in),

time: 127 us -> 127 us (level)
  waiting for transfers between devices: 10.2 us -> 8.73 us
    pallas_call x1, Pallas kernels: 2.62 us -> 0.91 us  [per_device(): call(functools.partial(rotate_mate_body, n_out, n_in, w_out), jax.ShapeDt...]
    pallas_call x1, Pallas kernels: 0.6 us -> 2.08 us  [per_device(): call(split_body, jax.ShapeDtypeStruct((2, w_out + w_in, bo.shape[0]), bf1...]
    all_to_all x1, waiting for transfers between devices: 10.2 us -> 8.72 us  [spread(): return lax.all_to_all(x, axes, split_axis=0, concat_axis=0, tiled=True)]
    pallas_call x1 -> x2, Pallas kernels: 2.81 us -> 2.93 us  [the longest x1 2.25 us: per_device(): call(functools.partial(restore_own_body, n_out, n_in, w_out), (jax.ShapeD...]
  transfers between devices with their start and end apart: 2 -> 2, of which waited for: 1 -> 1; matrix products, arithmetic and copies ran while one was open for 0% -> 0% of each run, Pallas kernels for 2% -> 4%
where the time goes in v5:
time: 127 us
  blocking collectives  80.7 us (64%)
  starting transfers between devices  19.9 us (16%)
  Pallas kernels  12.5 us (10%)
  waiting for transfers between devices  8.73 us (7%)
  local copies, waits for them, and re-layouts  3.19 us (3%)
    all_gather x1, blocking collectives, per_device(): codes = lax.all_gather(codes, ('y', 'xh', 'xl', 'c'), axis=0, tiled=True)  30.3 us
    all_to_all x1, blocking collectives, per_device(): lax.all_to_all(codes, ('z', 'xl'), split_axis=0, concat_axis=0, tiled=True)  20.4 us
    all_to_all x1, starting transfers between devices, spread(): return lax.all_to_all(x, axes, split_axis=0, concat_axis=0, tiled=True)  17.1 us
    all_to_all x1, blocking collectives, per_device(): codes = lax.all_to_all(codes, 'z', split_axis=0, concat_axis=0, tiled=True)  15.2 us
    all_to_all x1, blocking collectives, per_device(): parts = lax.all_to_all(part, GRP, split_axis=0, concat_axis=0, tiled=True)  14.7 us
    all_to_all x1, waiting for transfers between devices, spread(): return lax.all_to_all(x, axes, split_axis=0, concat_axis=0, tiled=True)  8.72 us
    pallas_call x1, Pallas kernels, per_device(): call(functools.partial(score_body, n_out, n_in, n_grp), jax.ShapeDtypeStr...  3.61 us
    ppermute x1, starting transfers between devices, per_device(): mate = lax.ppermute(own, 'c', [(0, 1), (1, 0)])  2.85 us
  transfers between devices with their start and end apart: 2, of which 1 were waited for; matrix products, arithmetic and copies ran while one was open for 0% of the time, Pallas kernels for 4%

profile of v5, /device:TPU:1, one launch (start us, length us, event | category | flops | bytes accessed | tf_op | source)
XLA Modules:
  0.0 126.6 jit_solution(9383888221514291758)
XLA Ops:
  0.0 0.8 maximum_reduce_fusion
  0.8 0.7 broadcast_in_dim.2
  1.5 17.1 %all-to-all-start = ((bf16[32,24,128]{2,1,0:T(8,128)(2,1)}), bf16[32,24,128]{2,1,0:T(8,128)(2,1)S(1)}, u32[]{:S(2)}, u32[]{:S(2)}) async-start(bf16[32,24,128]{2,1,0:T(8,128)(2,1)} %broadcast_in_dim.2), calls=%async_computation | async-start | bytes 393216 | tf_op jit(solution)/shard_map/all_to_all | solution.py:280
  18.6 0.0 copy-start.1
  18.6 1.4 %copy-done.1 = f32[1792,224]{0,1:T(8,128)S(1)} copy-done((f32[1792,224]{0,1:T(8,128)S(1)}, f32[1792,224]{0,1:T(8,128)}, u32[]{:S(2)}) %copy-start.1) | copy-done | bytes 1605656
  20.0 1.0 copy-done.3
  21.0 2.1 %shard_map.100.b_ref.own_ref = bf16[2,352,1792]{2,1,0:T(8,128)(2,1)} custom-call(f32[224,1792]{1,0:T(8,128)S(1)} %bitcast.6, f32[1024,128]{1,0:T(8,128)S(1)} %copy-done.3), custom_call_target="tpu_custom_call" | custom-call | tf_op jit(solution)/shard_map/pallas_call | solution.py:300
  23.1 2.9 %collective-permute-start = (bf16[2,352,1792]{2,1,0:T(8,128)(2,1)}, bf16[2,352,1792]{2,1,0:T(8,128)(2,1)S(1)}, u32[]{:S(2)}, u32[]{:S(2)}) collective-permute-start(bf16[2,352,1792]{2,1,0:T(8,128)(2,1)} %shard_map.100.b_ref.own_ref), channel_id=1, source_target_pairs={{0,1},{1,0},{2,3},{3,2},{4,5},{5,4},{6,7},{7,6},{8,9},{9,8},{10,11... | collective-permute-start | bytes 7569416 | tf_op jit(solution)/shard_map/ppermute | solution.py:303
  26.6 0.1 pad_add_fusion.at_ref
  26.7 8.7 %all-to-all-done.q_ref = bf16[32,24,128]{2,1,0:T(8,128)(2,1)S(1)} async-done(((bf16[32,24,128]{2,1,0:T(8,128)(2,1)}), bf16[32,24,128]{2,1,0:T(8,128)(2,1)S(1)}, u32[]{:S(2)}, u32[]{:S(2)}) %all-to-all-start) | async-done | bytes 196640 | tf_op jit(solution)/shard_map/all_to_all | solution.py:280
  35.4 0.0 copy-done.4
  35.4 2.7 %shard_map.101 = (bf16[32,2816]{1,0:T(8,128)(2,1)S(1)}, s16[32,384]{1,0:T(8,128)(2,1)S(1)}, f32[1,768]{1,0:T(1,128)S(1)}, s32[2,128]{1,0:T(2,128)S(1)}) custom-call(s32[2]{0:T(128)S(1)} %pad_add_fusion.at_ref, s32[2,64]{1,0:T(2,128)S(1)} %copy-done.6, s32[1]{0:T(128)S(6)} %copy.11.live_ref, f32[112,128]{1,0:T(8,128)S(1)} %bitcast.7, f32[64,128]{1,0:T(8,128)S(1)} %bitcast.8, ...), custom_call_target="tpu_custom_call" | custom-call | flops 20000000000 | tf_op jit(solution)/shard_map/pallas_call | solution.py:304
  38.1 0.0 collective-permute-done.b_ref.mate_ref
  38.1 0.9 shard_map.102
  39.0 14.7 %all_to_all.20.part_ref = s16[8,32,768]{2,1,0:T(8,128)(2,1)S(1)} all-to-all(s16[8,32,768]{2,1,0:T(8,128)(2,1)S(1)} %shard_map.102), channel_id=1, replica_groups=mesh['y'=4,'xh'=2,'z'=16,'xl'=2,'c'=2] {'y','xh'}, dimensions={0} | all-to-all | bytes 786432 | tf_op jit(solution)/shard_map/all_to_all | solution.py:322
  53.8 2.2 %shard_map.103 = (f32[32,2816]{1,0:T(8,128)S(1)}, bf16[64,256]{1,0:T(8,128)(2,1)S(1)}, bf16[64,128]{1,0:T(8,128)(2,1)S(1)}) custom-call(s16[8,32,768]{2,1,0:T(8,128)(2,1)S(1)} %all_to_all.20.part_ref, f32[1,768]{1,0:T(1,128)S(1)} %get-tuple-element.15.scale_ref, bf16[2,352,1792]{2,1,0:T(8,128)(2,1)} %shard_map.100.b_ref.own_ref), custom_call_target="tpu_custom_call" | custom-call | flops 20000000000 | tf_op jit(solution)/shard_map/pallas_call | solution.py:324
  56.0 0.7 shard_map.104
  56.7 0.0 copy-start
  56.7 0.0 copy-start.2
  56.7 20.4 %all_to_all.21.code_ref = s16[32,24,128]{2,1,0:T(8,128)(2,1)S(1)} all-to-all(s16[32,24,128]{2,1,0:T(8,128)(2,1)S(1)} %shard_map.104), channel_id=1, replica_groups=mesh['y'=4,'xh'=2,'z'=16,'xl'=2,'c'=2] {'z','xl'}, dimensions={0} | all-to-all | bytes 393216 | tf_op jit(solution)/shard_map/all_to_all | solution.py:340
  77.1 0.3 shard_map.105
  77.4 15.2 %all_to_all.22 = s16[16,24,128]{2,1,0:T(8,128)(2,1)S(1)} all-to-all(s16[16,24,128]{2,1,0:T(8,128)(2,1)S(1)} %shard_map.105), channel_id=1, replica_groups=mesh['y'=4,'xh'=2,'z'=16,'xl'=2,'c'=2] {'z'}, dimensions={0} | all-to-all | bytes 196608 | tf_op jit(solution)/shard_map/all_to_all | solution.py:345
  92.7 30.3 %all-gather.1.code_ref = s16[512,24,128]{2,1,0:T(8,128)(2,1)S(1)} all-gather(s16[16,24,128]{2,1,0:T(8,128)(2,1)S(1)} %all_to_all.22), channel_id=1, replica_groups=mesh['y'=4,'xh'=2,'z'=16,'xl'=2,'c'=2] {'y','xh','xl','c'}, dimensions={0}, use_global_device_ids=true | all-gather | bytes 3244032 | tf_op jit(solution)/shard_map/all_gather | solution.py:346
  123.0 3.6 %shard_map.106 = f32[2,2]{1,0:T(2,128)} custom-call(s32[2,128]{1,0:T(2,128)S(1)} %get-tuple-element.12.count_ref, s16[512,24,128]{2,1,0:T(8,128)(2,1)S(1)} %all-gather.1.code_ref, bf16[64,14336]{1,0:T(8,128)(2,1)S(1)} %copy-done, bf16[64,8192]{1,0:T(8,128)(2,1)S(1)} %copy-done.2), custom_call_target="tpu_custom_call" | custom-call | tf_op jit(solution)/shard_map/pallas_call | solution.py:347
  (9 shorter events, 0.0 us)
Async XLA Ops:
  1.5 34.0 %copy-start.4 = (f32[14336]{0:T(1024)S(1)}, f32[14336]{0:T(1024)}, u32[]{:S(2)}) copy-start(f32[14336]{0:T(1024)} %param.14) | copy-start | bytes 172036
  1.5 34.0 %copy-start.5 = (f32[8192]{0:T(1024)S(1)}, f32[8192]{0:T(1024)}, u32[]{:S(2)}) copy-start(f32[8192]{0:T(1024)} %param.15) | copy-start | bytes 98308
  1.5 34.0 %copy-start.6 = (s32[2,64]{1,0:T(2,128)S(1)}, s32[2,64]{1,0:T(2,128)}, u32[]{:S(2)}) copy-start(s32[2,64]{1,0:T(2,128)} %panel_ref.1) | copy-start | bytes 1540
  1.5 34.0 %all-to-all-start = ((bf16[32,24,128]{2,1,0:T(8,128)(2,1)}), bf16[32,24,128]{2,1,0:T(8,128)(2,1)S(1)}, u32[]{:S(2)}, u32[]{:S(2)}) async-start(bf16[32,24,128]{2,1,0:T(8,128)(2,1)} %broadcast_in_dim.2), calls=%async_computation | async-start | bytes 393216 | tf_op jit(solution)/shard_map/all_to_all | solution.py:280
  18.6 1.4 %copy-start.1 = (f32[1792,224]{0,1:T(8,128)S(1)}, f32[1792,224]{0,1:T(8,128)}, u32[]{:S(2)}) copy-start(f32[1792,224]{0,1:T(8,128)} %param.12) | copy-start | bytes 4816900
  20.0 1.0 copy-start.3
  23.1 15.0 %collective-permute-start = (bf16[2,352,1792]{2,1,0:T(8,128)(2,1)}, bf16[2,352,1792]{2,1,0:T(8,128)(2,1)S(1)}, u32[]{:S(2)}, u32[]{:S(2)}) collective-permute-start(bf16[2,352,1792]{2,1,0:T(8,128)(2,1)} %shard_map.100.b_ref.own_ref), channel_id=1, source_target_pairs={{0,1},{1,0},{2,3},{3,2},{4,5},{5,4},{6,7},{7,6},{8,9},{9,8},{10,11... | collective-permute-start | bytes 7569416 | tf_op jit(solution)/shard_map/ppermute | solution.py:303
  56.7 66.3 %copy-start = (bf16[64,14336]{1,0:T(8,128)(2,1)S(1)}, bf16[64,14336]{1,0:T(8,128)(2,1)}, u32[]{:S(2)}) copy-start(bf16[64,14336]{1,0:T(8,128)(2,1)} %to_ref.1) | copy-start | bytes 5505028
  56.7 66.3 %copy-start.2 = (bf16[64,8192]{1,0:T(8,128)(2,1)S(1)}, bf16[64,8192]{1,0:T(8,128)(2,1)}, u32[]{:S(2)}) copy-start(bf16[64,8192]{1,0:T(8,128)(2,1)} %ti_ref.1) | copy-start | bytes 3145732

commit v6 on v5

--- a/solution.py
+++ b/solution.py
@@ -221,7 +221,7 @@
         x = from_code(code_ref[j])
         a = x[n_out + n_in : n_out + n_in + 1]
         b = x[n_out + n_in + 1 : n_out + n_in + 2]
-        total = total + x * unit(jnp.where(is_out, a, b))
+        total = total + x * jnp.where(is_out, unit(a), unit(b))
     size = jnp.abs(total)
     steps_out = level(jnp.max(jnp.where(is_out, size, 0.0), keepdims=True))
     steps_in = level(jnp.max(jnp.where(is_in, size, 0.0), keepdims=True))

time: 127 us -> 127 us (level)
  no operation moved by 1% of the time
where the time goes in v6:
time: 127 us
  blocking collectives  80.7 us (64%)
  starting transfers between devices  19.9 us (16%)
  Pallas kernels  12.4 us (10%)
  waiting for transfers between devices  8.73 us (7%)
  local copies, waits for them, and re-layouts  3.19 us (3%)
    all_gather x1, blocking collectives, per_device(): codes = lax.all_gather(codes, ('y', 'xh', 'xl', 'c'), axis=0, tiled=True)  30.3 us
    all_to_all x1, blocking collectives, per_device(): lax.all_to_all(codes, ('z', 'xl'), split_axis=0, concat_axis=0, tiled=True)  20.4 us
    all_to_all x1, starting transfers between devices, spread(): return lax.all_to_all(x, axes, split_axis=0, concat_axis=0, tiled=True)  17.1 us
    all_to_all x1, blocking collectives, per_device(): codes = lax.all_to_all(codes, 'z', split_axis=0, concat_axis=0, tiled=True)  15.2 us
    all_to_all x1, blocking collectives, per_device(): parts = lax.all_to_all(part, GRP, split_axis=0, concat_axis=0, tiled=True)  14.7 us
    all_to_all x1, waiting for transfers between devices, spread(): return lax.all_to_all(x, axes, split_axis=0, concat_axis=0, tiled=True)  8.72 us
    pallas_call x1, Pallas kernels, per_device(): call(functools.partial(score_body, n_out, n_in, n_grp), jax.ShapeDtypeStr...  3.62 us
    ppermute x1, starting transfers between devices, per_device(): mate = lax.ppermute(own, 'c', [(0, 1), (1, 0)])  2.85 us
  transfers between devices with their start and end apart: 2, of which 1 were waited for; matrix products, arithmetic and copies ran while one was open for 0% of the time, Pallas kernels for 4%

profile of v6, /device:TPU:1, one launch (start us, length us, event | category | flops | bytes accessed | tf_op | source)
XLA Modules:
  0.0 126.6 jit_solution(15879691816730830904)
XLA Ops:
  0.0 0.8 maximum_reduce_fusion
  0.8 0.7 broadcast_in_dim.2
  1.5 17.1 %all-to-all-start = ((bf16[32,24,128]{2,1,0:T(8,128)(2,1)}), bf16[32,24,128]{2,1,0:T(8,128)(2,1)S(1)}, u32[]{:S(2)}, u32[]{:S(2)}) async-start(bf16[32,24,128]{2,1,0:T(8,128)(2,1)} %broadcast_in_dim.2), calls=%async_computation | async-start | bytes 393216 | tf_op jit(solution)/shard_map/all_to_all | solution.py:280
  18.6 0.0 copy-start.1
  18.6 1.4 %copy-done.1 = f32[1792,224]{0,1:T(8,128)S(1)} copy-done((f32[1792,224]{0,1:T(8,128)S(1)}, f32[1792,224]{0,1:T(8,128)}, u32[]{:S(2)}) %copy-start.1) | copy-done | bytes 1605656
  20.0 1.0 copy-done.3
  21.0 2.1 %shard_map.100.b_ref.own_ref = bf16[2,352,1792]{2,1,0:T(8,128)(2,1)} custom-call(f32[224,1792]{1,0:T(8,128)S(1)} %bitcast.6, f32[1024,128]{1,0:T(8,128)S(1)} %copy-done.3), custom_call_target="tpu_custom_call" | custom-call | tf_op jit(solution)/shard_map/pallas_call | solution.py:300
  23.1 2.9 %collective-permute-start = (bf16[2,352,1792]{2,1,0:T(8,128)(2,1)}, bf16[2,352,1792]{2,1,0:T(8,128)(2,1)S(1)}, u32[]{:S(2)}, u32[]{:S(2)}) collective-permute-start(bf16[2,352,1792]{2,1,0:T(8,128)(2,1)} %shard_map.100.b_ref.own_ref), channel_id=1, source_target_pairs={{0,1},{1,0},{2,3},{3,2},{4,5},{5,4},{6,7},{7,6},{8,9},{9,8},{10,11... | collective-permute-start | bytes 7569416 | tf_op jit(solution)/shard_map/ppermute | solution.py:303
  26.6 0.1 pad_add_fusion.at_ref
  26.7 8.7 %all-to-all-done.q_ref = bf16[32,24,128]{2,1,0:T(8,128)(2,1)S(1)} async-done(((bf16[32,24,128]{2,1,0:T(8,128)(2,1)}), bf16[32,24,128]{2,1,0:T(8,128)(2,1)S(1)}, u32[]{:S(2)}, u32[]{:S(2)}) %all-to-all-start) | async-done | bytes 196640 | tf_op jit(solution)/shard_map/all_to_all | solution.py:280
  35.4 0.0 copy-done.5
  35.4 2.7 %shard_map.101 = (bf16[32,2816]{1,0:T(8,128)(2,1)S(1)}, s16[32,384]{1,0:T(8,128)(2,1)S(1)}, f32[1,768]{1,0:T(1,128)S(1)}, s32[2,128]{1,0:T(2,128)S(1)}) custom-call(s32[2]{0:T(128)S(1)} %pad_add_fusion.at_ref, s32[2,64]{1,0:T(2,128)S(1)} %copy-done.6, s32[1]{0:T(128)S(6)} %copy.11.live_ref, f32[112,128]{1,0:T(8,128)S(1)} %bitcast.7, f32[64,128]{1,0:T(8,128)S(1)} %bitcast.8, ...), custom_call_target="tpu_custom_call" | custom-call | flops 20000000000 | tf_op jit(solution)/shard_map/pallas_call | solution.py:304
  38.1 0.0 collective-permute-done.b_ref.mate_ref
  38.1 0.9 shard_map.102
  39.0 14.7 %all_to_all.20.part_ref = s16[8,32,768]{2,1,0:T(8,128)(2,1)S(1)} all-to-all(s16[8,32,768]{2,1,0:T(8,128)(2,1)S(1)} %shard_map.102), channel_id=1, replica_groups=mesh['y'=4,'xh'=2,'z'=16,'xl'=2,'c'=2] {'y','xh'}, dimensions={0} | all-to-all | bytes 786432 | tf_op jit(solution)/shard_map/all_to_all | solution.py:322
  53.8 2.2 %shard_map.103 = (f32[32,2816]{1,0:T(8,128)S(1)}, bf16[64,256]{1,0:T(8,128)(2,1)S(1)}, bf16[64,128]{1,0:T(8,128)(2,1)S(1)}) custom-call(s16[8,32,768]{2,1,0:T(8,128)(2,1)S(1)} %all_to_all.20.part_ref, f32[1,768]{1,0:T(1,128)S(1)} %get-tuple-element.15.scale_ref, bf16[2,352,1792]{2,1,0:T(8,128)(2,1)} %shard_map.100.b_ref.own_ref), custom_call_target="tpu_custom_call" | custom-call | flops 20000000000 | tf_op jit(solution)/shard_map/pallas_call | solution.py:324
  56.0 0.7 shard_map.104
  56.7 0.0 copy-start
  56.7 0.0 copy-start.2
  56.7 20.4 %all_to_all.21.code_ref = s16[32,24,128]{2,1,0:T(8,128)(2,1)S(1)} all-to-all(s16[32,24,128]{2,1,0:T(8,128)(2,1)S(1)} %shard_map.104), channel_id=1, replica_groups=mesh['y'=4,'xh'=2,'z'=16,'xl'=2,'c'=2] {'z','xl'}, dimensions={0} | all-to-all | bytes 393216 | tf_op jit(solution)/shard_map/all_to_all | solution.py:340
  77.1 0.2 shard_map.105
  77.4 15.2 %all_to_all.22 = s16[16,24,128]{2,1,0:T(8,128)(2,1)S(1)} all-to-all(s16[16,24,128]{2,1,0:T(8,128)(2,1)S(1)} %shard_map.105), channel_id=1, replica_groups=mesh['y'=4,'xh'=2,'z'=16,'xl'=2,'c'=2] {'z'}, dimensions={0} | all-to-all | bytes 196608 | tf_op jit(solution)/shard_map/all_to_all | solution.py:345
  92.6 30.3 %all-gather.1.code_ref = s16[512,24,128]{2,1,0:T(8,128)(2,1)S(1)} all-gather(s16[16,24,128]{2,1,0:T(8,128)(2,1)S(1)} %all_to_all.22), channel_id=1, replica_groups=mesh['y'=4,'xh'=2,'z'=16,'xl'=2,'c'=2] {'y','xh','xl','c'}, dimensions={0}, use_global_device_ids=true | all-gather | bytes 3244032 | tf_op jit(solution)/shard_map/all_gather | solution.py:346
  122.9 3.6 %shard_map.106 = f32[2,2]{1,0:T(2,128)} custom-call(s32[2,128]{1,0:T(2,128)S(1)} %get-tuple-element.12.count_ref, s16[512,24,128]{2,1,0:T(8,128)(2,1)S(1)} %all-gather.1.code_ref, bf16[64,14336]{1,0:T(8,128)(2,1)S(1)} %copy-done, bf16[64,8192]{1,0:T(8,128)(2,1)S(1)} %copy-done.2), custom_call_target="tpu_custom_call" | custom-call | tf_op jit(solution)/shard_map/pallas_call | solution.py:347
  (9 shorter events, 0.0 us)
Async XLA Ops:
  1.5 34.0 %copy-start.4 = (f32[14336]{0:T(1024)S(1)}, f32[14336]{0:T(1024)}, u32[]{:S(2)}) copy-start(f32[14336]{0:T(1024)} %param.14) | copy-start | bytes 172036
  1.5 34.0 %copy-start.5 = (f32[8192]{0:T(1024)S(1)}, f32[8192]{0:T(1024)}, u32[]{:S(2)}) copy-start(f32[8192]{0:T(1024)} %param.15) | copy-start | bytes 98308
  1.5 34.0 %copy-start.6 = (s32[2,64]{1,0:T(2,128)S(1)}, s32[2,64]{1,0:T(2,128)}, u32[]{:S(2)}) copy-start(s32[2,64]{1,0:T(2,128)} %panel_ref.1) | copy-start | bytes 1540
  1.5 34.0 %all-to-all-start = ((bf16[32,24,128]{2,1,0:T(8,128)(2,1)}), bf16[32,24,128]{2,1,0:T(8,128)(2,1)S(1)}, u32[]{:S(2)}, u32[]{:S(2)}) async-start(bf16[32,24,128]{2,1,0:T(8,128)(2,1)} %broadcast_in_dim.2), calls=%async_computation | async-start | bytes 393216 | tf_op jit(solution)/shard_map/all_to_all | solution.py:280
  18.6 1.4 %copy-start.1 = (f32[1792,224]{0,1:T(8,128)S(1)}, f32[1792,224]{0,1:T(8,128)}, u32[]{:S(2)}) copy-start(f32[1792,224]{0,1:T(8,128)} %param.12) | copy-start | bytes 4816900
  20.0 1.0 copy-start.3
  23.1 15.0 %collective-permute-start = (bf16[2,352,1792]{2,1,0:T(8,128)(2,1)}, bf16[2,352,1792]{2,1,0:T(8,128)(2,1)S(1)}, u32[]{:S(2)}, u32[]{:S(2)}) collective-permute-start(bf16[2,352,1792]{2,1,0:T(8,128)(2,1)} %shard_map.100.b_ref.own_ref), channel_id=1, source_target_pairs={{0,1},{1,0},{2,3},{3,2},{4,5},{5,4},{6,7},{7,6},{8,9},{9,8},{10,11... | collective-permute-start | bytes 7569416 | tf_op jit(solution)/shard_map/ppermute | solution.py:303
  56.7 66.2 %copy-start = (bf16[64,14336]{1,0:T(8,128)(2,1)S(1)}, bf16[64,14336]{1,0:T(8,128)(2,1)}, u32[]{:S(2)}) copy-start(bf16[64,14336]{1,0:T(8,128)(2,1)} %to_ref.1) | copy-start | bytes 5505028
  56.7 66.2 %copy-start.2 = (bf16[64,8192]{1,0:T(8,128)(2,1)S(1)}, bf16[64,8192]{1,0:T(8,128)(2,1)}, u32[]{:S(2)}) copy-start(bf16[64,8192]{1,0:T(8,128)(2,1)} %ti_ref.1) | copy-start | bytes 3145732
